TPU v7x, 128 devices: a whole 4x4x4 slice. The times are simulated.
128 devices in a mesh: prow: 8 (over y, core), pcol: 16 (over z, x).
Axes of the slice: x: 4, y: 4, z: 4, core: 2. Of those that a mesh axis runs over, the one named last changes fastest.
Arguments:
- rhs_blocks: float32 [22, 2048, 512], P(None, 'prow'), may hold values from -6 to 6
- factor_tiles: bfloat16 [22, 2048, 6, 2048], P(None, 'prow', None, 'pcol'), may hold values from -0.0546875 to 0.0546875
- tile_scale: float32 [22, 6], replicated, may hold values from 0.5 to 2
- diag_inverse: bfloat16 [6, 2048, 2048], P(None, None, 'prow'), may hold values from -1.5 to 1.5, as said below
Outputs:
- solved_blocks: float32 [6, 2048, 512], P(None, 'pcol')
- trailing_rhs: float32 [16, 2048, 512], P(None, 'prow')
Inputs may be any that keep to these rules, and one draw needn't show every extreme that they name: `diag_inverse`: each block is zero above its diagonal.
All inputs are finite; a program needn't handle non-finite values.
Results may differ from a plain program's by a relative error of at most 0.0003.
Values sent between devices are 32-bit elements; how exact they have to be, the bound alone decides.
No kernel may reach another device: no remote copies, remote signals or barrier semaphores. Data moves between devices by JAX's collectives and lax.ppermute only.
A program may use at most 192 MiB of HBM per device.

v0:
```python
import jax
import jax.numpy as jnp
from jax import lax
from jax.sharding import PartitionSpec as P


def on_device(rhs_blocks, factor_tiles, tile_scale, diag_inverse):
    block_count = rhs_blocks.shape[0]
    step_count = factor_tiles.shape[2]
    column_width = factor_tiles.shape[3]
    column_index = lax.axis_index("pcol")
    blocks = jnp.arange(block_count)
    partial_value = jnp.zeros(rhs_blocks.shape, jnp.float32)
    solved = []
    for column in range(step_count):
        inverse = diag_inverse[column].astype(jnp.float32)
        remainder = rhs_blocks[column] - lax.psum(partial_value[column], "pcol")
        inverse_rows = lax.dynamic_slice_in_dim(
            inverse, column_index * column_width, column_width, 0
        )
        product = jnp.dot(inverse_rows, remainder, precision=lax.Precision.HIGHEST)
        solved_rows = lax.psum(product, "prow")
        weights = tile_scale[:, column] * (blocks > column).astype(jnp.float32)
        scaled_tiles = factor_tiles[:, :, column, :].astype(jnp.float32) * weights[:, None, None]
        partial_value = partial_value + jnp.einsum(
            "sqj,jr->sqr", scaled_tiles, solved_rows, precision=lax.Precision.HIGHEST
        )
        solved.append(solved_rows)
    trailing = rhs_blocks[step_count:] - lax.psum(partial_value[step_count:], "pcol")
    return (jnp.stack(solved), trailing)


def solution(mesh):
    in_specs = (P(None, "prow", None), P(None, "prow", None, "pcol"), P(), P(None, None, "prow"))
    out_specs = (P(None, "pcol", None), P(None, "prow", None))
    return jax.shard_map(
        on_device, mesh=mesh, in_specs=in_specs, out_specs=out_specs, check_vma=False
    )
```

profile of v0, /device:TPU:6, one launch (start us, length us, event | category | flops | bytes accessed | tf_op | source)
XLA Modules:
  0.0 1080.8 jit_solution(18229035820466916130)
XLA Ops:
  7.2 4.6 fusion.57
  11.8 2.1 fusion.25
  14.1 62.2 %all-reduce.13.cloned.1.call-done = f32[128,512]{1,0:T(8,128)} async-done(((f32[128,512]{1,0:T(8,128)}), f32[128,512]{1,0:T(8,128)}) %all-reduce.13.cloned.1.call-update) | async-done | bytes 262160 | tf_op jit(solution)/shard_map/psum | solution.py:22
  76.3 11.4 %fusion.1 = f32[22,256,512]{2,1,0:T(8,128)S(1)} fusion(f32[22]{0:T(128)S(1)} %get-tuple-element.12, bf16[22,256,6,128]{3,1,2,0:T(8,128)(2,1)} %param.5, f32[128,512]{1,0:T(8,128)} %all-reduce.13.cloned.1.call-done), kind=kOutput, calls=%fused_computation.13 | convolution fusion | flops 4430626816 | bytes 13238360 | tf_op jit(solution)/shard_map/sqj,jr->sqr/dot_general | solution.py:25
  87.8 4.3 copy-done
  92.1 0.8 slice_bitcast_fusion.4
  93.0 84.1 %all-reduce.15.cloned.1.call-done = f32[256,512]{1,0:T(8,128)} async-done(((f32[256,512]{1,0:T(8,128)}), f32[256,512]{1,0:T(8,128)}) %all-reduce.15.cloned.1.call-update) | async-done | bytes 524304 | tf_op jit(solution)/shard_map/psum | solution.py:17
  177.1 2.3 fusion.24
  179.4 0.2 all-reduce.19.cloned.1.call-start
  179.6 59.4 %all-reduce.17.cloned.1.call-done = f32[128,512]{1,0:T(8,128)} async-done(((f32[128,512]{1,0:T(8,128)}), f32[128,512]{1,0:T(8,128)}) %all-reduce.17.cloned.1.call-update) | async-done | bytes 262160 | tf_op jit(solution)/shard_map/psum | solution.py:22
  239.0 12.9 %convolution_add_fusion.3 = f32[22,256,512]{2,1,0:T(8,128)S(1)} fusion(f32[22,256,512]{2,1,0:T(8,128)} %copy-done, f32[22]{0:T(128)S(1)} %get-tuple-element.11, bf16[22,256,6,128]{3,1,2,0:T(8,128)(2,1)} %param.5, f32[128,512]{1,0:T(8,128)} %all-reduce.17.cloned.1.call-done), kind=kOutput, calls=%fused_computation.5 | convolution fusion | flops 4433510400 | bytes 24772696 | tf_op jit(solution)/shard_map/sqj,jr->sqr/dot_general | solution.py:25
  251.9 4.3 copy-done.1
  256.3 0.8 slice_bitcast_fusion.3
  257.1 0.0 all-reduce.21.cloned.1.call-start
  257.2 84.1 %all-reduce.19.cloned.1.call-done = f32[256,512]{1,0:T(8,128)} async-done(((f32[256,512]{1,0:T(8,128)}), f32[256,512]{1,0:T(8,128)}) %all-reduce.19.cloned.1.call-update) | async-done | bytes 524304 | tf_op jit(solution)/shard_map/psum | solution.py:17
  341.2 2.3 fusion.23
  343.6 0.0 all-reduce.23.cloned.1.call-start
  343.6 59.9 %all-reduce.21.cloned.1.call-done = f32[128,512]{1,0:T(8,128)} async-done(((f32[128,512]{1,0:T(8,128)}), f32[128,512]{1,0:T(8,128)}) %all-reduce.21.cloned.1.call-update) | async-done | bytes 262160 | tf_op jit(solution)/shard_map/psum | solution.py:22
  403.5 12.9 %convolution_add_fusion.2 = f32[22,256,512]{2,1,0:T(8,128)S(1)} fusion(f32[22,256,512]{2,1,0:T(8,128)} %copy-done.1, f32[22]{0:T(128)S(1)} %get-tuple-element.10, bf16[22,256,6,128]{3,1,2,0:T(8,128)(2,1)} %param.5, f32[128,512]{1,0:T(8,128)} %all-reduce.21.cloned.1.call-done), kind=kOutput, calls=%fused_computation.4 | convolution fusion | flops 4433510400 | bytes 24772696 | tf_op jit(solution)/shard_map/sqj,jr->sqr/dot_general | solution.py:25
  416.4 4.3 copy-done.2
  420.8 0.8 slice_bitcast_fusion.2
  421.7 84.1 %all-reduce.23.cloned.1.call-done = f32[256,512]{1,0:T(8,128)} async-done(((f32[256,512]{1,0:T(8,128)}), f32[256,512]{1,0:T(8,128)}) %all-reduce.23.cloned.1.call-update) | async-done | bytes 524304 | tf_op jit(solution)/shard_map/psum | solution.py:17
  505.8 2.3 fusion.22
  508.0 0.3 all-reduce.27.cloned.1.call-start
  508.3 59.9 %all-reduce.25.cloned.1.call-done = f32[128,512]{1,0:T(8,128)} async-done(((f32[128,512]{1,0:T(8,128)}), f32[128,512]{1,0:T(8,128)}) %all-reduce.25.cloned.1.call-update) | async-done | bytes 262160 | tf_op jit(solution)/shard_map/psum | solution.py:22
  568.2 12.9 %convolution_add_fusion.1 = f32[22,256,512]{2,1,0:T(8,128)S(1)} fusion(f32[22,256,512]{2,1,0:T(8,128)} %copy-done.2, f32[22]{0:T(128)S(1)} %get-tuple-element.9, bf16[22,256,6,128]{3,1,2,0:T(8,128)(2,1)} %param.5, f32[128,512]{1,0:T(8,128)} %all-reduce.25.cloned.1.call-done), kind=kOutput, calls=%fused_computation.3 | convolution fusion | flops 4433510400 | bytes 24772696 | tf_op jit(solution)/shard_map/sqj,jr->sqr/dot_general | solution.py:25
  581.1 4.3 copy-done.3
  585.4 0.8 slice_bitcast_fusion.1
  586.3 84.1 %all-reduce.27.cloned.1.call-done = f32[256,512]{1,0:T(8,128)} async-done(((f32[256,512]{1,0:T(8,128)}), f32[256,512]{1,0:T(8,128)}) %all-reduce.27.cloned.1.call-update) | async-done | bytes 524304 | tf_op jit(solution)/shard_map/psum | solution.py:17
  670.4 2.3 fusion.21
  672.8 60.1 %all-reduce.29.cloned.1.call-done = f32[128,512]{1,0:T(8,128)} async-done(((f32[128,512]{1,0:T(8,128)}), f32[128,512]{1,0:T(8,128)}) %all-reduce.29.cloned.1.call-update) | async-done | bytes 262160 | tf_op jit(solution)/shard_map/psum | solution.py:22
  732.9 12.9 %convolution_add_fusion = f32[22,256,512]{2,1,0:T(8,128)S(1)} fusion(f32[22,256,512]{2,1,0:T(8,128)} %copy-done.3, f32[22]{0:T(128)S(1)} %get-tuple-element.13, bf16[22,256,6,128]{3,1,2,0:T(8,128)(2,1)} %param.5, f32[128,512]{1,0:T(8,128)} %all-reduce.29.cloned.1.call-done), kind=kOutput, calls=%fused_computation.2 | convolution fusion | flops 4433510400 | bytes 24772696 | tf_op jit(solution)/shard_map/sqj,jr->sqr/dot_general | solution.py:25
  745.8 4.3 copy-done.4
  750.1 0.8 slice_bitcast_fusion
  751.0 84.1 %all-reduce.31.cloned.1.call-done = f32[256,512]{1,0:T(8,128)} async-done(((f32[256,512]{1,0:T(8,128)}), f32[256,512]{1,0:T(8,128)}) %all-reduce.31.cloned.1.call-update) | async-done | bytes 524304 | tf_op jit(solution)/shard_map/psum | solution.py:17
  835.1 2.3 fusion.20
  837.4 0.3 all-reduce.35.cloned.1.call-start
  837.7 59.9 %all-reduce.33.cloned.1.call-done = f32[128,512]{1,0:T(8,128)} async-done(((f32[128,512]{1,0:T(8,128)}), f32[128,512]{1,0:T(8,128)}) %all-reduce.33.cloned.1.call-update) | async-done | bytes 262160 | tf_op jit(solution)/shard_map/psum | solution.py:22
  897.5 13.0 %fusion = f32[22,256,512]{2,1,0:T(8,128)} fusion(f32[22]{0:T(128)S(1)} %get-tuple-element.8, bf16[22,256,6,128]{3,1,2,0:T(8,128)(2,1)} %param.5, f32[128,512]{1,0:T(8,128)} %all-reduce.33.cloned.1.call-done), kind=kOutput, calls=%fused_computation.7 | convolution fusion | flops 4430626816 | bytes 13238360 | tf_op jit(solution)/shard_map/sqj,jr->sqr/dot_general | solution.py:25
  910.6 11.8 %slice_add_fusion = f32[16,256,512]{2,1,0:T(8,128)} fusion(f32[22,256,512]{2,1,0:T(8,128)} %fusion, f32[22,256,512]{2,1,0:T(8,128)} %copy-done.4), kind=kLoop, calls=%fused_computation | loop fusion | flops 2097152 | bytes 25165824 | tf_op jit(solution)/shard_map/add | solution.py:25
  922.4 0.9 copy-done.9
  923.3 0.1 copy-done.5
  923.4 0.1 copy-done.6
  923.5 0.1 copy-done.7
  923.5 0.1 copy-done.8
  923.6 0.1 copy-done.10
  923.7 138.3 %all-reduce.35.cloned.1.call-done = f32[16,256,512]{2,1,0:T(8,128)} async-done(((f32[16,256,512]{2,1,0:T(8,128)}), f32[16,256,512]{2,1,0:T(8,128)}) %all-reduce.35.cloned.1.call-update) | async-done | bytes 8388624 | tf_op jit(solution)/shard_map/psum | solution.py:29
  1062.0 11.6 %slice_subtract_fusion = f32[16,256,512]{2,1,0:T(8,128)} fusion(f32[16,256,512]{2,1,0:T(8,128)} %all-reduce.35.cloned.1.call-done, f32[22,256,512]{2,1,0:T(8,128)} %param.4), kind=kLoop, calls=%fused_computation.1 | loop fusion | flops 2097152 | bytes 25165824 | tf_op jit(solution)/shard_map/sub | solution.py:29
  (41 shorter events, 0.6 us)
Async XLA Ops:
  7.2 6.9 copy-start.12
  7.2 69.1 %all-reduce.13.cloned.1.call-start = ((), (), s32[]{:S(2)}) async-start(), calls=%async_computation | async-start | bytes 524288 | tf_op jit(solution)/shard_map/psum | solution.py:22
  14.0 163.1 %all-reduce.15.cloned.1.call-start = ((), (), s32[]{:S(2)}) async-start(), calls=%async_computation.1 | async-start | bytes 1048576 | tf_op jit(solution)/shard_map/psum | solution.py:17
  87.7 4.3 copy-start
  92.9 146.1 %all-reduce.17.cloned.1.call-start = ((), (), s32[]{:S(2)}) async-start(), calls=%async_computation.2 | async-start | bytes 524288 | tf_op jit(solution)/shard_map/psum | solution.py:22
  179.4 161.9 %all-reduce.19.cloned.1.call-start = ((), (), s32[]{:S(2)}) async-start(), calls=%async_computation.3 | async-start | bytes 1048576 | tf_op jit(solution)/shard_map/psum | solution.py:17
  251.9 4.3 copy-start.1
  257.1 146.4 %all-reduce.21.cloned.1.call-start = ((), (), s32[]{:S(2)}) async-start(), calls=%async_computation.4 | async-start | bytes 524288 | tf_op jit(solution)/shard_map/psum | solution.py:22
  343.6 162.2 %all-reduce.23.cloned.1.call-start = ((), (), s32[]{:S(2)}) async-start(), calls=%async_computation.5 | async-start | bytes 1048576 | tf_op jit(solution)/shard_map/psum | solution.py:17
  416.4 4.3 copy-start.2
  421.6 146.6 %all-reduce.25.cloned.1.call-start = ((), (), s32[]{:S(2)}) async-start(), calls=%async_computation.6 | async-start | bytes 524288 | tf_op jit(solution)/shard_map/psum | solution.py:22
  508.0 162.4 %all-reduce.27.cloned.1.call-start = ((), (), s32[]{:S(2)}) async-start(), calls=%async_computation.7 | async-start | bytes 1048576 | tf_op jit(solution)/shard_map/psum | solution.py:17
  581.1 4.3 copy-start.3
  586.3 146.6 %all-reduce.29.cloned.1.call-start = ((), (), s32[]{:S(2)}) async-start(), calls=%async_computation.8 | async-start | bytes 524288 | tf_op jit(solution)/shard_map/psum | solution.py:22
  672.7 162.4 %all-reduce.31.cloned.1.call-start = ((), (), s32[]{:S(2)}) async-start(), calls=%async_computation.9 | async-start | bytes 1048576 | tf_op jit(solution)/shard_map/psum | solution.py:17
  745.8 4.3 copy-start.4
  750.9 146.6 %all-reduce.33.cloned.1.call-start = ((), (), s32[]{:S(2)}) async-start(), calls=%async_computation.10 | async-start | bytes 524288 | tf_op jit(solution)/shard_map/psum | solution.py:22
  837.4 224.6 %all-reduce.35.cloned.1.call-start = ((), (), s32[]{:S(2)}) async-start(), calls=%async_computation.11 | async-start | bytes 16777216 | tf_op jit(solution)/shard_map/psum | solution.py:29
  922.3 0.9 copy-start.9
  922.3 1.0 copy-start.5
  922.3 1.1 copy-start.6
  922.3 1.2 copy-start.7
  922.3 1.3 copy-start.8
  922.3 1.3 copy-start.10
  923.7 149.9 %copy-start.11 = (f32[6,128,512]{2,1,0:T(8,128)}, f32[6,128,512]{2,1,0:T(8,128)S(1)}, u32[]{:S(2)}) copy-start(f32[6,128,512]{2,1,0:T(8,128)S(1)} %bitcast_dynamic-update-slice_fusion) | copy-start | bytes 4718596
Sparse Core Ops, SparseCore 0:
  14.1 62.1 all-reduce.12
  93.0 83.9 all-reduce.14
  179.5 59.4 all-reduce.16
  257.2 83.9 all-reduce.18
  344.0 59.5 all-reduce.20
  421.7 83.9 all-reduce.22
  508.6 59.5 all-reduce.24
  586.4 83.9 all-reduce.26
  673.3 59.5 all-reduce.28
  751.1 83.9 all-reduce.30
  838.0 59.5 all-reduce.32
  922.5 139.4 all-reduce.34
where the time goes:
time: 1090 us; the launch traced here: 1080 us
  waiting for transfers between devices  920 us (84%)
  matrix products  89.5 us (8%)
  local copies, waits for them, and re-layouts  31.6 us (3%)
  other arithmetic  23.4 us (2%)
  between operations  14.8 us (1%)
    psum x5, waiting for transfers between devices, on_device(): remainder = rhs_blocks[column] - lax.psum(partial_value[column], 'pcol')  420 us
    psum x6, waiting for transfers between devices, on_device(): solved_rows = lax.psum(product, 'prow')  361 us
    psum x1, waiting for transfers between devices, on_device(): lax.psum(partial_value[step_count:], 'pcol')  138 us
    dot_general x6, matrix products, on_device(): jnp.einsum('sqj,jr->sqr', scaled_tiles, solved_rows, precision=lax.Precis...  76 us
    unnamed x31, local copies, waits for them, and re-layouts  22.9 us
  transfers between devices with their start and end apart: 12, of which 12 were waited for; matrix products, arithmetic and copies ran while one was open for 0% of the time, Pallas kernels for 0%

commit v1 on v0

v1 whole, which is shorter than its diff:
```python
import functools

import jax
import jax.numpy as jnp
from jax import lax
from jax.experimental import pallas as pl
from jax.experimental.pallas import tpu as pltpu
from jax.sharding import PartitionSpec as P

F32 = jnp.float32
BF16 = jnp.bfloat16
STEPS = 6
PAIRS = (((1, 0),), ((2, 0), (2, 1), (3, 0), (3, 1), (3, 2)), tuple((s, j) for s in (4, 5) for j in range(s)))


def split(value):
    high = value.astype(BF16)
    return high, (value - high.astype(F32)).astype(BF16)


def dot(a, b):
    return jnp.dot(a, b, preferred_element_type=F32)


def dot3(a, b):
    a_high, a_low = split(a)
    b_high, b_low = split(b)
    return dot(a_high, b_high) + (dot(a_high, b_low) + dot(a_low, b_high))


def full(shape):
    return pl.BlockSpec(shape, lambda *_: (0,) * len(shape))


def params(mib):
    return pltpu.CompilerParams(vmem_limit_bytes=mib << 20)


def store_gram(meta, product, keep, send, at):
    x, y, u = meta[0], meta[1], meta[2]
    for zz in range(4):
        for ex in range(4):
            chunk = zz * 4 + lax.rem(x + ex, 4)
            for ey in range(4):
                row = (chunk * 8 + lax.rem(y + ey, 4) * 2) * 16
                keep[ey, at + ex * 4 + zz] = product[pl.ds(pl.multiple_of(row + u * 16, 16), 16), :]
                send[ey, at + ex * 4 + zz] = product[pl.ds(pl.multiple_of(row + (1 - u) * 16, 16), 16), :]


def first_kernel(meta, scale, inverse, rhs, tile, keep, send, product):
    x, y, u, z = meta[0], meta[1], meta[2], meta[3]
    product[pl.ds(0, 2048), :] = dot(inverse[1], tile[0, 0]) * scale[1, 0]
    store_gram(meta, product, keep, send, 24)
    for s in range(STEPS):
        high, low = split(rhs[s])
        both = jnp.concatenate([high, low], axis=0)
        for dz in range(4):
            chunk = lax.rem(z + 4 - dz, 4) * 4 + x
            rows = inverse[s, pl.ds(pl.multiple_of(chunk * 128, 128), 128), :]
            base = (s * 4 + dz) * 128
            product[pl.ds(base, 128), :] = dot(jnp.concatenate([rows, rows], axis=1), both)
            for ey in range(4):
                row = base + lax.rem(y + ey, 4) * 32
                keep[ey, s * 4 + dz] = product[pl.ds(pl.multiple_of(row + u * 16, 16), 16), :]
                send[ey, s * 4 + dz] = product[pl.ds(pl.multiple_of(row + (1 - u) * 16, 16), 16), :]


def first_products(meta, scale, inverse, rhs, tiles):
    out = jax.ShapeDtypeStruct((4, 40, 16, 128), F32)
    return pl.pallas_call(
        first_kernel,
        grid_spec=pltpu.PrefetchScalarGridSpec(
            num_scalar_prefetch=2,
            grid=(1,),
            in_specs=[
                full((6, 2048, 256)),
                pl.BlockSpec((6, 256, 128), lambda i, m, s: (0, 0, m[3])),
                pl.BlockSpec((1, 1, 256, 128), lambda i, m, s: (1, 0, 0, 0)),
            ],
            out_specs=[full((4, 40, 16, 128))] * 2,
            scratch_shapes=[pltpu.VMEM((3072, 128), F32)],
        ),
        out_shape=[out, out],
        compiler_params=params(40),
        name="first_products",
    )(meta, scale, inverse, rhs, tiles)


def gram_kernel(meta, scale, blocks, inverse, tile, keep, send, product):
    i = pl.program_id(0)
    s, j = blocks[2 * i], blocks[2 * i + 1]
    product[...] = dot(inverse[0], tile[0, 0]) * scale[s, j]
    store_gram(meta, product, keep, send, 0)


def gram_products(meta, scale, inverse, tiles, pairs):
    count = len(pairs)
    out = jax.ShapeDtypeStruct((4, 16 * count, 16, 128), F32)
    block = pl.BlockSpec((4, 16, 16, 128), lambda i, m, s, b: (0, i, 0, 0))
    return pl.pallas_call(
        gram_kernel,
        grid_spec=pltpu.PrefetchScalarGridSpec(
            num_scalar_prefetch=3,
            grid=(count,),
            in_specs=[
                pl.BlockSpec((1, 2048, 256), lambda i, m, s, b: (b[2 * i], 0, 0)),
                pl.BlockSpec((1, 1, 256, 128), lambda i, m, s, b: (b[2 * i], b[2 * i + 1], 0, 0)),
            ],
            out_specs=[block, block],
            scratch_shapes=[pltpu.VMEM((2048, 128), F32)],
        ),
        out_shape=[out, out],
        compiler_params=params(24),
        name="gram_products",
    )(meta, scale, jnp.array([v for pair in pairs for v in pair], jnp.int32), inverse, tiles)


def step_kernel(count, meta, *refs):
    y, u = meta[1], meta[2]
    pieces, refs = refs[:4], refs[4:]
    older, refs = refs[: count - 1], refs[count - 1 :]
    gram, refs = refs[: 4 * count], refs[4 * count :]
    chunks, solved = refs[:4], refs[4]
    for ey in range(4):
        row = lax.rem(y + 4 - ey, 4) * 32
        for eu in range(2):
            at = pl.multiple_of(row + (u + eu - 2 * u * eu) * 16, 16)
            for dz in range(4):
                solved[dz, pl.ds(at, 16), :] = pieces[ey][eu, dz]
    total = jnp.zeros((256, 128), F32)
    for j in range(count):
        block = jnp.concatenate([ref[...].reshape(256, 128) for ref in gram[4 * j : 4 * j + 4]], axis=1)
        source = solved if j == count - 1 else older[j]
        total = total + dot3(block, source[...].reshape(512, 128))
    total = total.reshape(4, 4, 16, 128)
    for ex in range(4):
        chunks[ex][...] = total[ex]


def step(meta, pieces, older, gram):
    count = len(older) + 1
    specs = [full((2, 4, 16, 128))] * 4 + [full((4, 128, 128))] * len(older)
    operands = list(pieces) + list(older)
    for arrays, at in gram:
        for array in arrays:
            specs.append(pl.BlockSpec((16, 16, 128), functools.partial(lambda i, m, at: (at, 0, 0), at=at)))
            operands.append(array)
    return pl.pallas_call(
        functools.partial(step_kernel, count),
        grid_spec=pltpu.PrefetchScalarGridSpec(
            num_scalar_prefetch=1,
            grid=(1,),
            in_specs=specs,
            out_specs=[full((4, 16, 128))] * 4 + [full((4, 128, 128))],
        ),
        out_shape=[jax.ShapeDtypeStruct((4, 16, 128), F32)] * 4 + [jax.ShapeDtypeStruct((4, 128, 128), F32)],
        compiler_params=params(32),
        name="step",
    )(meta, *operands)


def last_kernel(meta, a, b, c, d, solved):
    y, u = meta[1], meta[2]
    for ey, piece in enumerate((a, b, c, d)):
        row = lax.rem(y + 4 - ey, 4) * 32
        for eu in range(2):
            at = pl.multiple_of(row + (u + eu - 2 * u * eu) * 16, 16)
            for dz in range(4):
                solved[dz, pl.ds(at, 16), :] = piece[eu, dz]


def last(meta, pieces):
    return pl.pallas_call(
        last_kernel,
        grid_spec=pltpu.PrefetchScalarGridSpec(
            num_scalar_prefetch=1, grid=(1,), in_specs=[full((2, 4, 16, 128))] * 4, out_specs=full((4, 128, 128))
        ),
        out_shape=jax.ShapeDtypeStruct((4, 128, 128), F32),
        name="last",
    )(meta, *pieces)


def sum_kernel(meta, a, b, c, d, start, out):
    z = meta[3]
    for dz in range(4):
        at = lax.rem(z + 4 - dz, 4)
        out[dz] = start[dz] - ((a[at] + b[at]) + (c[at] + d[at]))


def sum_x(meta, chunks, start, s):
    return pl.pallas_call(
        sum_kernel,
        grid_spec=pltpu.PrefetchScalarGridSpec(
            num_scalar_prefetch=1,
            grid=(1,),
            in_specs=[full((4, 16, 128))] * 4 + [pl.BlockSpec((4, 16, 128), lambda i, m: (s, 0, 0))],
            out_specs=full((4, 16, 128)),
        ),
        out_shape=jax.ShapeDtypeStruct((4, 16, 128), F32),
        name="sum_x",
    )(meta, *chunks, start)


def columns_kernel(count, meta, a, b, c, d, solved, both):
    z = meta[3]
    for k in range(count):
        for dz, piece in enumerate((a, b, c, d)):
            at = pl.multiple_of(lax.rem(z + 4 - dz, 4) * 128, 128)
            solved[k, :, pl.ds(at, 128)] = piece[k]
        high, low = split(solved[k])
        both[k, pl.ds(0, 128), :] = high
        both[k, pl.ds(128, 128), :] = low


def columns(meta, pieces):
    count = pieces[0].shape[0]
    return pl.pallas_call(
        functools.partial(columns_kernel, count),
        grid_spec=pltpu.PrefetchScalarGridSpec(
            num_scalar_prefetch=1,
            grid=(1,),
            in_specs=[full((count, 128, 128))] * 4,
            out_specs=[full((count, 128, 512)), full((count, 256, 512))],
        ),
        out_shape=[jax.ShapeDtypeStruct((count, 128, 512), F32), jax.ShapeDtypeStruct((count, 256, 512), BF16)],
        compiler_params=params(16),
        name="columns",
    )(meta, *pieces)


def trail_kernel(steps, blocks, scale, tile, both, *refs):
    i = pl.program_id(0)
    s = blocks[0] + i
    total = None if len(refs) == 1 else refs[0][0]
    for n, k in enumerate(steps):
        own = tile[0, n]
        part = dot(jnp.concatenate([own, own], axis=1), both[n]) * scale[s, k]
        total = part if total is None else total + part
    refs[-1][0] = total


def trail(first, scale, tiles, both, steps, total=None):
    count = 6 if len(steps) > 1 else 1
    k = steps[0] // count
    chunk = pl.BlockSpec((1, 256, 512), lambda i, b, s: (i, 0, 0))
    specs = [pl.BlockSpec((1, count, 256, 128), lambda i, b, s: (b[0] + i, k, 0, 0)), full(both.shape)]
    operands = [tiles, both]
    if total is not None:
        specs.append(chunk)
        operands.append(total)
    return pl.pallas_call(
        functools.partial(trail_kernel, steps),
        grid_spec=pltpu.PrefetchScalarGridSpec(num_scalar_prefetch=2, grid=(2,), in_specs=specs, out_specs=chunk),
        out_shape=jax.ShapeDtypeStruct((2, 256, 512), F32),
        compiler_params=params(24),
        name="trail",
    )(first, scale, *operands)


def sum_sub_kernel(me, a, b, c, d, *outs):
    for e in range(4):
        at = lax.rem(me[0] + e, 4)
        outs[e][...] = (a[at] + b[at]) + (c[at] + d[at])


def sum_sub(me, parts):
    return pl.pallas_call(
        sum_sub_kernel,
        grid_spec=pltpu.PrefetchScalarGridSpec(
            num_scalar_prefetch=1,
            grid=(1,),
            in_specs=[full((4, 128, 512))] * 4,
            out_specs=[full((128, 512))] * 4,
        ),
        out_shape=[jax.ShapeDtypeStruct((128, 512), F32)] * 4,
        compiler_params=params(24),
        name="sum_sub",
    )(me, *parts)


def finish_kernel(at, rhs, a, b, c, d, out):
    out[...] = rhs[0] - ((a[...] + b[...]) + (c[...] + d[...]))


def finish(at, rhs, parts):
    return pl.pallas_call(
        finish_kernel,
        grid_spec=pltpu.PrefetchScalarGridSpec(
            num_scalar_prefetch=1,
            grid=(1,),
            in_specs=[pl.BlockSpec((1, 128, 512), lambda i, at: (at[0], at[1], 0))] + [full((128, 512))] * 4,
            out_specs=full((128, 512)),
        ),
        out_shape=jax.ShapeDtypeStruct((128, 512), F32),
        name="finish",
    )(at, rhs, *parts)


def place_kernel(me, a, b, c, d, out):
    for e, piece in enumerate((a, b, c, d)):
        out[lax.rem(me[0] + 4 - e, 4)] = piece[...]


def place(me, parts):
    return pl.pallas_call(
        place_kernel,
        grid_spec=pltpu.PrefetchScalarGridSpec(
            num_scalar_prefetch=1, grid=(1,), in_specs=[full((128, 512))] * 4, out_specs=full((4, 128, 512))
        ),
        out_shape=jax.ShapeDtypeStruct((4, 128, 512), F32),
        name="place",
    )(me, *parts)


def on_device(rhs_blocks, factor_tiles, tile_scale, diag_inverse):
    row, column = lax.axis_index("prow"), lax.axis_index("pcol")
    y, u, z, x = row // 2, row % 2, column // 4, column % 4
    meta = jnp.stack([x, y, u, z]).astype(jnp.int32)
    tiles = jnp.transpose(factor_tiles, (0, 2, 1, 3))

    def shift(value, axis, d):
        if axis == "x":
            return lax.ppermute(value, "pcol", [(i, i // 4 * 4 + (i + d) % 4) for i in range(16)])
        if axis == "z":
            return lax.ppermute(value, "pcol", [(i, (i + 4 * d) % 16) for i in range(16)])
        if axis == "y":
            return lax.ppermute(value, "prow", [(i, (i + 2 * d) % 8) for i in range(8)])
        return lax.ppermute(value, "prow", [(i, i ^ 1) for i in range(8)])

    def exchange(values, axis):
        return [values[0]] + [shift(values[d], axis, d) for d in (1, 2, 3)]

    def spread(value, axis):
        return exchange([value] * 4, axis)

    def reduce_rows(keep, send):
        half = keep + shift(send, "core", 1)
        a, b, c, d = exchange([half[i] for i in range(4)], "y")
        return (a + b) + (c + d)

    def gather(piece):
        both = jnp.stack([piece, shift(piece, "core", 1)])
        return spread(both, "y")

    first = reduce_rows(*first_products(meta, tile_scale, diag_inverse, rhs_blocks, tiles))
    start = first[:24]
    grams = {(1, 0): (spread(first[24:], "z"), 0)}
    for pairs in PAIRS[1:]:
        total = reduce_rows(*gram_products(meta, tile_scale, diag_inverse, tiles, pairs))
        arrays = spread(total, "z")
        for n, pair in enumerate(pairs):
            grams[pair] = (arrays, n)

    solved = []
    piece = start[:4]
    for s in range(1, STEPS):
        *chunks, latest = step(meta, gather(piece), solved, [grams[s, j] for j in range(s)])
        solved.append(latest)
        piece = sum_x(meta, exchange(chunks, "x"), start, s)
    latest = last(meta, gather(piece))

    early = exchange([jnp.stack([v[-d % 4] for v in solved]) for d in range(4)], "z")
    solved_early, both_early = columns(meta, early)
    late = exchange([latest[-d % 4][None] for d in range(4)], "z")
    solved_late, both_late = columns(meta, late)

    halves = []
    for half, (one, two, me, other) in enumerate((("x", "z", x, z), ("z", "x", z, x))):
        base = 6 + 8 * half
        firsts = [(base + 2 * ((me + d) % 4)).astype(jnp.int32)[None] for d in range(4)]
        parts = [trail(at, tile_scale, tiles, both_early, range(5)) for at in firsts]
        parts = [trail(at, tile_scale, tiles, both_late, (5,), p) for at, p in zip(firsts, parts)]
        parts = [v.reshape(4, 128, 512) for v in exchange(parts, one)]
        subs = exchange(sum_sub(other.astype(jnp.int32)[None], parts), two)
        at = jnp.stack([base + 2 * me + other // 2, other % 2]).astype(jnp.int32)
        done = finish(at, rhs_blocks, subs)
        chunk = place(other.astype(jnp.int32)[None], spread(done, two)).reshape(2, 256, 512)
        halves.append((8 * half, me, spread(chunk, one)))
    trailing = jnp.zeros((16, 256, 512), F32)
    for base, me, chunks in halves:
        for d, chunk in enumerate(chunks):
            trailing = lax.dynamic_update_slice(trailing, chunk, (base + 2 * ((me - d) % 4), 0, 0))
    return jnp.concatenate([solved_early, solved_late]), trailing


def solution(mesh):
    in_specs = (P(None, "prow", None), P(None, "prow", None, "pcol"), P(), P(None, None, "prow"))
    out_specs = (P(None, "pcol", None), P(None, "prow", None))
    return jax.shard_map(
        on_device, mesh=mesh, in_specs=in_specs, out_specs=out_specs, check_vma=False
    )
```

time: 1090 us -> 667 us (0.61)
  waiting for transfers between devices: 920 us -> 375 us
  starting transfers between devices: 1.13 us -> 112 us
  matrix products: 89.5 us -> 0 us
  Pallas kernels: 0 us -> 82.9 us
  local copies, waits for them, and re-layouts: 31.6 us -> 68.5 us
  between operations: 14.8 us -> 1.92 us
    psum x12 -> x0, waiting for transfers between devices: 920 us -> none  [the longest x5 420 us: on_device(): remainder = rhs_blocks[column] - lax.psum(partial_value[column], 'pcol')]
    ppermute x0 -> x90, waiting for transfers between devices: none -> 375 us  [the longest x27 139 us: shift(): lax.ppermute(value, 'pcol', [(i, (i + 4 * d) % 16) for i in range(16)])]
    ppermute x0 -> x90, starting transfers between devices: none -> 112 us  [the longest x27 47.4 us: shift(): lax.ppermute(value, 'pcol', [(i, (i + 4 * d) % 16) for i in range(16)])]
    dot_general x12 -> x0, matrix products: 89.5 us -> none  [the longest x6 76 us: on_device(): jnp.einsum('sqj,jr->sqr', scaled_tiles, solved_rows, precision=lax.Precis...]
    pallas_call x0 -> x38, Pallas kernels: none -> 82.9 us  [the longest x16 29.1 us: trail(): pl.pallas_call(functools.partial(trail_kernel, steps), grid_spec=pltpu.Pr...]
    unnamed x31 -> x169, local copies, waits for them, and re-layouts: 22.9 us -> 56.9 us
    sub x1 -> x0, other arithmetic: 11.6 us -> none  [on_device(): rhs_blocks[step_count:] - lax.psum(partial_value[step_count:], 'pcol')]
  transfers between devices with their start and end apart: 12 -> 90, of which waited for: 12 -> 51; matrix products, arithmetic and copies ran while one was open for 0% -> 4% of each run, Pallas kernels for 0% -> 9%
where the time goes in v1:
time: 667 us; the launch traced here: 656 us
  waiting for transfers between devices  375 us (56%)
  starting transfers between devices  112 us (17%)
  Pallas kernels  82.9 us (12%)
  local copies, waits for them, and re-layouts  68.5 us (10%)
  other arithmetic  15.7 us (2%)
    ppermute x27, waiting for transfers between devices, shift(): lax.ppermute(value, 'pcol', [(i, (i + 4 * d) % 16) for i in range(16)])  139 us
    ppermute x27, waiting for transfers between devices, shift(): lax.ppermute(value, 'pcol', [(i, i // 4 * 4 + (i + d) % 4) for i in range...  133 us
    ppermute x27, waiting for transfers between devices, shift(): return lax.ppermute(value, 'prow', [(i, (i + 2 * d) % 8) for i in range(8)])  92.6 us
    unnamed x169, local copies, waits for them, and re-layouts  56.9 us
    ppermute x27, starting transfers between devices, shift(): lax.ppermute(value, 'pcol', [(i, (i + 4 * d) % 16) for i in range(16)])  47.4 us
    ppermute x27, starting transfers between devices, shift(): lax.ppermute(value, 'pcol', [(i, i // 4 * 4 + (i + d) % 4) for i in range...  32.3 us
    ppermute x27, starting transfers between devices, shift(): return lax.ppermute(value, 'prow', [(i, (i + 2 * d) % 8) for i in range(8)])  31.2 us
    pallas_call x16, Pallas kernels, trail(): pl.pallas_call(functools.partial(trail_kernel, steps), grid_spec=pltpu.Pr...  29.1 us
  transfers between devices with their start and end apart: 90, of which 51 were waited for; matrix products, arithmetic and copies ran while one was open for 4% of the time, Pallas kernels for 9%

profile of v1, /device:TPU:6, one launch (start us, length us, event | category | flops | bytes accessed | tf_op | source)
XLA Modules:
  0.0 656.2 jit_solution(5116677153718270673)
XLA Ops:
  1.5 3.5 copy-done
  8.4 6.2 gram_products.3
  14.7 3.7 gram_products.2
  19.0 3.3 first_products.1
  22.4 5.8 collective-permute-done
  34.4 5.2 collective-permute-done.1
  39.5 8.2 %collective-permute-done.2 = f32[40,16,128]{2,1,0:T(8,128)S(1)} collective-permute-done((f32[40,16,128]{2,1,0:T(8,128)S(1)}, f32[40,16,128]{2,1,0:T(8,128)S(1)}, u32[]{:S(2)}, u32[]{:S(2)}) %collective-permute-start.2) | collective-permute-done | bytes 327712 | tf_op jit(solution)/shard_map/ppermute | solution.py:327
  51.5 4.1 collective-permute-start.10
  60.7 3.1 add.211
  63.9 4.9 collective-permute-done.5.refs_1_
  71.3 3.9 collective-permute-start.9
  84.8 9.6 %collective-permute-done.20 = f32[80,16,128]{2,1,0:T(8,128)S(1)} collective-permute-done((f32[80,16,128]{2,1,0:T(8,128)S(1)}, f32[80,16,128]{2,1,0:T(8,128)S(1)}, u32[]{:S(2)}, u32[]{:S(2)}) %collective-permute-start.20) | collective-permute-done | bytes 655392 | tf_op jit(solution)/shard_map/ppermute | solution.py:327
  94.8 12.4 %collective-permute-done.21 = f32[80,16,128]{2,1,0:T(8,128)S(1)} collective-permute-done((f32[80,16,128]{2,1,0:T(8,128)S(1)}, f32[80,16,128]{2,1,0:T(8,128)S(1)}, u32[]{:S(2)}, u32[]{:S(2)}) %collective-permute-start.21) | collective-permute-done | bytes 655392 | tf_op jit(solution)/shard_map/ppermute | solution.py:327
  109.7 4.0 collective-permute-done.12.c
  115.6 3.6 collective-permute-done.13.d
  125.2 18.7 %collective-permute-done.15.refs_1_ = f32[2,4,16,128]{3,2,1,0:T(8,128)S(1)} collective-permute-done((f32[2,4,16,128]{3,2,1,0:T(8,128)S(1)}, f32[2,4,16,128]{3,2,1,0:T(8,128)S(1)}, u32[]{:S(2)}, u32[]{:S(2)}) %collective-permute-start.15) | collective-permute-done | bytes 65568 | tf_op jit(solution)/shard_map/ppermute | solution.py:327
  145.7 10.6 %collective-permute-done.42 = f32[144,16,128]{2,1,0:T(8,128)} collective-permute-done((f32[144,16,128]{2,1,0:T(8,128)S(1)}, f32[144,16,128]{2,1,0:T(8,128)}, u32[]{:S(2)}, u32[]{:S(2)}) %collective-permute-start.42) | collective-permute-done | bytes 1179680 | tf_op jit(solution)/shard_map/ppermute | solution.py:327
  164.8 32.7 %collective-permute-done.24.refs_8_.refs_12_.refs_9_.refs_13_.refs_17_ = f32[80,16,128]{2,1,0:T(8,128)S(1)} collective-permute-done((f32[80,16,128]{2,1,0:T(8,128)}, f32[80,16,128]{2,1,0:T(8,128)S(1)}, u32[]{:S(2)}, u32[]{:S(2)}) %collective-permute-start.24) | collective-permute-done | bytes 655392 | tf_op jit(solution)/shard_map/ppermute | solution.py:325
  207.0 3.1 collective-permute-done.27.d
  215.0 6.8 %collective-permute-done.29.refs_1_ = f32[2,4,16,128]{3,2,1,0:T(8,128)S(1)} collective-permute-done((f32[2,4,16,128]{3,2,1,0:T(8,128)S(1)}, f32[2,4,16,128]{3,2,1,0:T(8,128)S(1)}, u32[]{:S(2)}, u32[]{:S(2)}) %collective-permute-start.29) | collective-permute-done | bytes 65568 | tf_op jit(solution)/shard_map/ppermute | solution.py:327
  221.8 4.3 collective-permute-done.31.refs_3_
  251.3 4.1 collective-permute-done.36.refs_1_
  255.4 4.3 collective-permute-done.38.refs_3_
  289.9 3.0 step.9
  297.1 3.3 collective-permute-done.57.c
  312.1 5.5 collective-permute-start.54
  324.4 9.4 %collective-permute-done.63.b = f32[1,128,128]{2,1,0:T(8,128)S(1)} collective-permute-done((f32[1,128,128]{2,1,0:T(8,128)S(1)}, f32[1,128,128]{2,1,0:T(8,128)S(1)}, u32[]{:S(2)}, u32[]{:S(2)}) %collective-permute-start.63) | collective-permute-done | bytes 65568 | tf_op jit(solution)/shard_map/ppermute | solution.py:325
  343.1 3.4 copy-done.1
  361.7 3.5 copy-done.2
  368.2 28.5 %collective-permute-done.68 = f32[2,256,512]{2,1,0:T(8,128)} collective-permute-done((f32[2,256,512]{2,1,0:T(8,128)}, f32[2,256,512]{2,1,0:T(8,128)}, u32[]{:S(2)}, u32[]{:S(2)}) %collective-permute-start.68) | collective-permute-done | bytes 1048608 | tf_op jit(solution)/shard_map/ppermute | solution.py:323
  396.7 4.5 collective-permute-done.66
  404.9 3.4 copy-done.3
  416.9 3.7 collective-permute-start.79
  429.9 37.0 %collective-permute-done.70.c = f32[128,512]{1,0:T(8,128)} collective-permute-done((f32[128,512]{1,0:T(8,128)S(1)}, f32[128,512]{1,0:T(8,128)}, u32[]{:S(2)}, u32[]{:S(2)}) %collective-permute-start.70) | collective-permute-done | bytes 262176 | tf_op jit(solution)/shard_map/ppermute | solution.py:325
  466.9 9.0 %collective-permute-done.71.d = f32[128,512]{1,0:T(8,128)} collective-permute-done((f32[128,512]{1,0:T(8,128)S(1)}, f32[128,512]{1,0:T(8,128)}, u32[]{:S(2)}, u32[]{:S(2)}) %collective-permute-start.71) | collective-permute-done | bytes 262176 | tf_op jit(solution)/shard_map/ppermute | solution.py:325
  478.6 3.0 collective-permute-start.72
  482.7 5.9 collective-permute-done.72.b
  490.6 4.1 collective-permute-done.73.c
  498.2 3.7 collective-permute-start.75
  501.9 3.5 copy-done.4
  513.9 20.6 %collective-permute-done.81.b = f32[128,512]{1,0:T(8,128)S(1)} collective-permute-done((f32[128,512]{1,0:T(8,128)S(1)}, f32[128,512]{1,0:T(8,128)S(1)}, u32[]{:S(2)}, u32[]{:S(2)}) %collective-permute-start.81) | collective-permute-done | bytes 262176 | tf_op jit(solution)/shard_map/ppermute | solution.py:323
  538.2 3.7 collective-permute-start.84
  545.5 27.2 %collective-permute-done.84.b = f32[128,512]{1,0:T(8,128)S(1)} collective-permute-done((f32[128,512]{1,0:T(8,128)}, f32[128,512]{1,0:T(8,128)S(1)}, u32[]{:S(2)}, u32[]{:S(2)}) %collective-permute-start.84) | collective-permute-done | bytes 262176 | tf_op jit(solution)/shard_map/ppermute | solution.py:323
  574.2 20.4 %collective-permute-done.85.c = f32[128,512]{1,0:T(8,128)S(1)} collective-permute-done((f32[128,512]{1,0:T(8,128)}, f32[128,512]{1,0:T(8,128)S(1)}, u32[]{:S(2)}, u32[]{:S(2)}) %collective-permute-start.85) | collective-permute-done | bytes 262176 | tf_op jit(solution)/shard_map/ppermute | solution.py:323
  600.3 5.0 collective-permute-start.88
  614.4 12.4 %collective-permute-done.87 = f32[2,256,512]{2,1,0:T(8,128)} collective-permute-done((f32[2,256,512]{2,1,0:T(8,128)}, f32[2,256,512]{2,1,0:T(8,128)}, u32[]{:S(2)}, u32[]{:S(2)}) %collective-permute-start.87) | collective-permute-done | bytes 1048608 | tf_op jit(solution)/shard_map/ppermute | solution.py:325
  628.2 22.8 %collective-permute-done.88 = f32[2,256,512]{2,1,0:T(8,128)} collective-permute-done((f32[2,256,512]{2,1,0:T(8,128)}, f32[2,256,512]{2,1,0:T(8,128)}, u32[]{:S(2)}, u32[]{:S(2)}) %collective-permute-start.88) | collective-permute-done | bytes 1048608 | tf_op jit(solution)/shard_map/ppermute | solution.py:325
  652.4 3.4 copy-done.47
  (373 shorter events, 238.5 us)
Async XLA Ops:
  14.6 44.5 %collective-permute-start.39 = (f32[4,144,16,128]{3,2,1,0:T(8,128)S(1)}, f32[4,144,16,128]{3,2,1,0:T(8,128)}, u32[]{:S(2)}, u32[]{:S(2)}) collective-permute-start(f32[4,144,16,128]{3,2,1,0:T(8,128)S(1)} %get-tuple-element.65), channel_id=1, source_target_pairs={{0,16},{16,0},{32,48},{48,32},{64,80},{80,64},{96,112},{112,96},{1... | collective-permute-start | bytes 14155784 | tf_op jit(solution)/shard_map/ppermute | solution.py:328
  18.5 29.4 %collective-permute-start.18 = (f32[4,80,16,128]{3,2,1,0:T(8,128)S(1)}, f32[4,80,16,128]{3,2,1,0:T(8,128)}, u32[]{:S(2)}, u32[]{:S(2)}) collective-permute-start(f32[4,80,16,128]{3,2,1,0:T(8,128)S(1)} %get-tuple-element.53), channel_id=1, source_target_pairs={{0,16},{16,0},{32,48},{48,32},{64,80},{80,64},{96,112},{112,96},{1... | collective-permute-start | bytes 7864328 | tf_op jit(solution)/shard_map/ppermute | solution.py:328
  30.1 17.6 %collective-permute-start.2 = (f32[40,16,128]{2,1,0:T(8,128)S(1)}, f32[40,16,128]{2,1,0:T(8,128)S(1)}, u32[]{:S(2)}, u32[]{:S(2)}) collective-permute-start(f32[40,16,128]{2,1,0:T(8,128)S(1)} %get-tuple-element.95), channel_id=1, source_target_pairs={{0,64},{16,80},{32,96},{48,112},{64,0},{80,16},{96,32},{112,48},{1... | collective-permute-start | bytes 983048 | tf_op jit(solution)/shard_map/ppermute | solution.py:327
  33.0 14.8 %collective-permute-start.3 = (f32[40,16,128]{2,1,0:T(8,128)S(1)}, f32[40,16,128]{2,1,0:T(8,128)S(1)}, u32[]{:S(2)}, u32[]{:S(2)}) collective-permute-start(f32[40,16,128]{2,1,0:T(8,128)S(1)} %get-tuple-element.94), channel_id=1, source_target_pairs={{0,96},{16,112},{32,0},{48,16},{64,32},{80,48},{96,64},{112,80},{1... | collective-permute-start | bytes 983048 | tf_op jit(solution)/shard_map/ppermute | solution.py:327
  50.2 30.9 %collective-permute-start.19 = (f32[80,16,128]{2,1,0:T(8,128)S(1)}, f32[80,16,128]{2,1,0:T(8,128)S(1)}, u32[]{:S(2)}, u32[]{:S(2)}) collective-permute-start(f32[80,16,128]{2,1,0:T(8,128)S(1)} %get-tuple-element.93), channel_id=1, source_target_pairs={{0,32},{16,48},{32,64},{48,80},{64,96},{80,112},{96,0},{112,16},{1... | collective-permute-start | bytes 1966088 | tf_op jit(solution)/shard_map/ppermute | solution.py:327
  51.5 24.6 %collective-permute-start.10 = (f32[16,16,128]{2,1,0:T(8,128)S(1)}, f32[16,16,128]{2,1,0:T(8,128)S(1)}, u32[]{:S(2)}, u32[]{:S(2)}) collective-permute-start(f32[16,16,128]{2,1,0:T(8,128)S(1)} %slice.162.refs_4_), channel_id=1, source_target_pairs={{0,12},{1,13},{2,14},{3,15},{4,0},{5,1},{6,2},{7,3},{8,4},{9,5},{1... | collective-permute-start | bytes 393224 | tf_op jit(solution)/shard_map/ppermute | solution.py:325
  55.6 13.2 %collective-permute-start.5 = (f32[2,4,16,128]{3,2,1,0:T(8,128)S(1)}, f32[2,4,16,128]{3,2,1,0:T(8,128)S(1)}, u32[]{:S(2)}, u32[]{:S(2)}) collective-permute-start(f32[2,4,16,128]{3,2,1,0:T(8,128)S(1)} %pad_maximum_fusion.1.refs_0_), channel_id=1, source_target_pairs={{0,32},{16,48},{32,64},{48,80},{64,96},{80,112},{96,0},{112,16},{1... | collective-permute-start | bytes 196616 | tf_op jit(solution)/shard_map/ppermute | solution.py:327
  57.0 14.3 %collective-permute-start.6 = (f32[2,4,16,128]{3,2,1,0:T(8,128)S(1)}, f32[2,4,16,128]{3,2,1,0:T(8,128)S(1)}, u32[]{:S(2)}, u32[]{:S(2)}) collective-permute-start(f32[2,4,16,128]{3,2,1,0:T(8,128)S(1)} %pad_maximum_fusion.1.refs_0_), channel_id=1, source_target_pairs={{0,64},{16,80},{32,96},{48,112},{64,0},{80,16},{96,32},{112,48},{1... | collective-permute-start | bytes 196616 | tf_op jit(solution)/shard_map/ppermute | solution.py:327
  59.2 16.0 %collective-permute-start.7 = (f32[2,4,16,128]{3,2,1,0:T(8,128)S(1)}, f32[2,4,16,128]{3,2,1,0:T(8,128)S(1)}, u32[]{:S(2)}, u32[]{:S(2)}) collective-permute-start(f32[2,4,16,128]{3,2,1,0:T(8,128)S(1)} %pad_maximum_fusion.1.refs_0_), channel_id=1, source_target_pairs={{0,96},{16,112},{32,0},{48,16},{64,32},{80,48},{96,64},{112,80},{1... | collective-permute-start | bytes 196616 | tf_op jit(solution)/shard_map/ppermute | solution.py:327
  75.2 19.2 %collective-permute-start.20 = (f32[80,16,128]{2,1,0:T(8,128)S(1)}, f32[80,16,128]{2,1,0:T(8,128)S(1)}, u32[]{:S(2)}, u32[]{:S(2)}) collective-permute-start(f32[80,16,128]{2,1,0:T(8,128)S(1)} %get-tuple-element.92), channel_id=1, source_target_pairs={{0,64},{16,80},{32,96},{48,112},{64,0},{80,16},{96,32},{112,48},{1... | collective-permute-start | bytes 1966088 | tf_op jit(solution)/shard_map/ppermute | solution.py:327
  76.1 31.1 %collective-permute-start.21 = (f32[80,16,128]{2,1,0:T(8,128)S(1)}, f32[80,16,128]{2,1,0:T(8,128)S(1)}, u32[]{:S(2)}, u32[]{:S(2)}) collective-permute-start(f32[80,16,128]{2,1,0:T(8,128)S(1)} %get-tuple-element.91), channel_id=1, source_target_pairs={{0,96},{16,112},{32,0},{48,16},{64,32},{80,48},{96,64},{112,80},{1... | collective-permute-start | bytes 1966088 | tf_op jit(solution)/shard_map/ppermute | solution.py:327
  77.9 66.3 %collective-permute-start.40 = (f32[144,16,128]{2,1,0:T(8,128)S(1)}, f32[144,16,128]{2,1,0:T(8,128)}, u32[]{:S(2)}, u32[]{:S(2)}) collective-permute-start(f32[144,16,128]{2,1,0:T(8,128)S(1)} %get-tuple-element.90), channel_id=1, source_target_pairs={{0,32},{16,48},{32,64},{48,80},{64,96},{80,112},{96,0},{112,16},{1... | collective-permute-start | bytes 3538952 | tf_op jit(solution)/shard_map/ppermute | solution.py:327
  79.1 66.3 %collective-permute-start.41 = (f32[144,16,128]{2,1,0:T(8,128)S(1)}, f32[144,16,128]{2,1,0:T(8,128)}, u32[]{:S(2)}, u32[]{:S(2)}) collective-permute-start(f32[144,16,128]{2,1,0:T(8,128)S(1)} %get-tuple-element.89), channel_id=1, source_target_pairs={{0,64},{16,80},{32,96},{48,112},{64,0},{80,16},{96,32},{112,48},{1... | collective-permute-start | bytes 3538952 | tf_op jit(solution)/shard_map/ppermute | solution.py:327
  81.0 75.2 %collective-permute-start.42 = (f32[144,16,128]{2,1,0:T(8,128)S(1)}, f32[144,16,128]{2,1,0:T(8,128)}, u32[]{:S(2)}, u32[]{:S(2)}) collective-permute-start(f32[144,16,128]{2,1,0:T(8,128)S(1)} %get-tuple-element.88), channel_id=1, source_target_pairs={{0,96},{16,112},{32,0},{48,16},{64,32},{80,48},{96,64},{112,80},{1... | collective-permute-start | bytes 3538952 | tf_op jit(solution)/shard_map/ppermute | solution.py:327
  94.3 13.9 %collective-permute-start.11 = (f32[4,16,128]{2,1,0:T(8,128)S(1)}, f32[4,16,128]{2,1,0:T(8,128)S(1)}, u32[]{:S(2)}, u32[]{:S(2)}) collective-permute-start(f32[4,16,128]{2,1,0:T(8,128)S(1)} %get-tuple-element.49), channel_id=1, source_target_pairs={{0,1},{1,2},{2,3},{3,0},{4,5},{5,6},{6,7},{7,4},{8,9},{9,10},{10,1... | collective-permute-start | bytes 98312 | tf_op jit(solution)/shard_map/ppermute | solution.py:323
  108.2 53.2 %collective-permute-start.22 = (f32[80,16,128]{2,1,0:T(8,128)}, f32[80,16,128]{2,1,0:T(8,128)}, u32[]{:S(2)}, u32[]{:S(2)}) collective-permute-start(f32[80,16,128]{2,1,0:T(8,128)} %fusion.3.refs_5_.refs_9_.refs_6_.refs_10_.refs_14_), channel_id=1, source_target_pairs={{0,4},{1,5},{2,6},{3,7},{4,8},{5,9},{6,10},{7,11},{8,12},{9,13},{1... | collective-permute-start | bytes 1966088 | tf_op jit(solution)/shard_map/ppermute | solution.py:325
  124.1 19.8 %collective-permute-start.15 = (f32[2,4,16,128]{3,2,1,0:T(8,128)S(1)}, f32[2,4,16,128]{3,2,1,0:T(8,128)S(1)}, u32[]{:S(2)}, u32[]{:S(2)}) collective-permute-start(f32[2,4,16,128]{3,2,1,0:T(8,128)S(1)} %pad_maximum_fusion.2.refs_0_), channel_id=1, source_target_pairs={{0,32},{16,48},{32,64},{48,80},{64,96},{80,112},{96,0},{112,16},{1... | collective-permute-start | bytes 196616 | tf_op jit(solution)/shard_map/ppermute | solution.py:327
  143.9 16.0 %collective-permute-start.16 = (f32[2,4,16,128]{3,2,1,0:T(8,128)S(1)}, f32[2,4,16,128]{3,2,1,0:T(8,128)S(1)}, u32[]{:S(2)}, u32[]{:S(2)}) collective-permute-start(f32[2,4,16,128]{3,2,1,0:T(8,128)S(1)} %pad_maximum_fusion.2.refs_0_), channel_id=1, source_target_pairs={{0,64},{16,80},{32,96},{48,112},{64,0},{80,16},{96,32},{112,48},{1... | collective-permute-start | bytes 196616 | tf_op jit(solution)/shard_map/ppermute | solution.py:327
  144.2 16.8 %collective-permute-start.17 = (f32[2,4,16,128]{3,2,1,0:T(8,128)S(1)}, f32[2,4,16,128]{3,2,1,0:T(8,128)S(1)}, u32[]{:S(2)}, u32[]{:S(2)}) collective-permute-start(f32[2,4,16,128]{3,2,1,0:T(8,128)S(1)} %pad_maximum_fusion.2.refs_0_), channel_id=1, source_target_pairs={{0,96},{16,112},{32,0},{48,16},{64,32},{80,48},{96,64},{112,80},{1... | collective-permute-start | bytes 196616 | tf_op jit(solution)/shard_map/ppermute | solution.py:327
  145.4 19.4 %collective-permute-start.23 = (f32[80,16,128]{2,1,0:T(8,128)}, f32[80,16,128]{2,1,0:T(8,128)S(1)}, u32[]{:S(2)}, u32[]{:S(2)}) collective-permute-start(f32[80,16,128]{2,1,0:T(8,128)} %fusion.3.refs_5_.refs_9_.refs_6_.refs_10_.refs_14_), channel_id=1, source_target_pairs={{0,8},{1,9},{2,10},{3,11},{4,12},{5,13},{6,14},{7,15},{8,0},{9,1},... | collective-permute-start | bytes 1966088 | tf_op jit(solution)/shard_map/ppermute | solution.py:325
  156.2 41.3 %collective-permute-start.24 = (f32[80,16,128]{2,1,0:T(8,128)}, f32[80,16,128]{2,1,0:T(8,128)S(1)}, u32[]{:S(2)}, u32[]{:S(2)}) collective-permute-start(f32[80,16,128]{2,1,0:T(8,128)} %fusion.3.refs_5_.refs_9_.refs_6_.refs_10_.refs_14_), channel_id=1, source_target_pairs={{0,12},{1,13},{2,14},{3,15},{4,0},{5,1},{6,2},{7,3},{8,4},{9,5},{1... | collective-permute-start | bytes 1966088 | tf_op jit(solution)/shard_map/ppermute | solution.py:325
  159.9 99.7 %collective-permute-start.43 = (f32[144,16,128]{2,1,0:T(8,128)S(1)}, f32[144,16,128]{2,1,0:T(8,128)S(1)}, u32[]{:S(2)}, u32[]{:S(2)}) collective-permute-start(f32[144,16,128]{2,1,0:T(8,128)S(1)} %fusion.1.refs_7_.refs_11_.refs_15_.refs_19_.refs_8_.refs_12_.refs_16_.refs_20_.refs_24_), channel_id=1, source_target_pairs={{0,4},{1,5},{2,6},{3,7},{4,8},{5,9},{6,10},{7,11},{8,12},{9,13},{1... | collective-permute-start | bytes 3538952 | tf_op jit(solution)/shard_map/ppermute | solution.py:325
  161.0 98.6 %collective-permute-start.44 = (f32[144,16,128]{2,1,0:T(8,128)S(1)}, f32[144,16,128]{2,1,0:T(8,128)S(1)}, u32[]{:S(2)}, u32[]{:S(2)}) collective-permute-start(f32[144,16,128]{2,1,0:T(8,128)S(1)} %fusion.1.refs_7_.refs_11_.refs_15_.refs_19_.refs_8_.refs_12_.refs_16_.refs_20_.refs_24_), channel_id=1, source_target_pairs={{0,8},{1,9},{2,10},{3,11},{4,12},{5,13},{6,14},{7,15},{8,0},{9,1},... | collective-permute-start | bytes 3538952 | tf_op jit(solution)/shard_map/ppermute | solution.py:325
  161.4 98.2 %collective-permute-start.45 = (f32[144,16,128]{2,1,0:T(8,128)S(1)}, f32[144,16,128]{2,1,0:T(8,128)}, u32[]{:S(2)}, u32[]{:S(2)}) collective-permute-start(f32[144,16,128]{2,1,0:T(8,128)S(1)} %fusion.1.refs_7_.refs_11_.refs_15_.refs_19_.refs_8_.refs_12_.refs_16_.refs_20_.refs_24_), channel_id=1, source_target_pairs={{0,12},{1,13},{2,14},{3,15},{4,0},{5,1},{6,2},{7,3},{8,4},{9,5},{1... | collective-permute-start | bytes 3538952 | tf_op jit(solution)/shard_map/ppermute | solution.py:325
  312.1 27.3 %collective-permute-start.53 = (f32[5,128,128]{2,1,0:T(8,128)}, f32[5,128,128]{2,1,0:T(8,128)S(1)}, u32[]{:S(2)}, u32[]{:S(2)}) collective-permute-start(f32[5,128,128]{2,1,0:T(8,128)} %get-tuple-element.101), channel_id=1, source_target_pairs={{0,4},{1,5},{2,6},{3,7},{4,8},{5,9},{6,10},{7,11},{8,12},{9,13},{1... | collective-permute-start | bytes 983048 | tf_op jit(solution)/shard_map/ppermute | solution.py:325
  312.1 27.3 %collective-permute-start.54 = (f32[5,128,128]{2,1,0:T(8,128)}, f32[5,128,128]{2,1,0:T(8,128)S(1)}, u32[]{:S(2)}, u32[]{:S(2)}) collective-permute-start(f32[5,128,128]{2,1,0:T(8,128)} %get-tuple-element.100), channel_id=1, source_target_pairs={{0,8},{1,9},{2,10},{3,11},{4,12},{5,13},{6,14},{7,15},{8,0},{9,1},... | collective-permute-start | bytes 983048 | tf_op jit(solution)/shard_map/ppermute | solution.py:325
  317.6 21.8 %collective-permute-start.55 = (f32[5,128,128]{2,1,0:T(8,128)}, f32[5,128,128]{2,1,0:T(8,128)S(1)}, u32[]{:S(2)}, u32[]{:S(2)}) collective-permute-start(f32[5,128,128]{2,1,0:T(8,128)} %get-tuple-element.99), channel_id=1, source_target_pairs={{0,12},{1,13},{2,14},{3,15},{4,0},{5,1},{6,2},{7,3},{8,4},{9,5},{1... | collective-permute-start | bytes 983048 | tf_op jit(solution)/shard_map/ppermute | solution.py:325
  350.4 46.3 %collective-permute-start.68 = (f32[2,256,512]{2,1,0:T(8,128)}, f32[2,256,512]{2,1,0:T(8,128)}, u32[]{:S(2)}, u32[]{:S(2)}) collective-permute-start(f32[2,256,512]{2,1,0:T(8,128)} %trail.23), channel_id=1, source_target_pairs={{0,3},{1,0},{2,1},{3,2},{4,7},{5,4},{6,5},{7,6},{8,11},{9,8},{10,9... | collective-permute-start | bytes 3145736 | tf_op jit(solution)/shard_map/ppermute | solution.py:323
  354.2 42.5 %collective-permute-start.67 = (f32[2,256,512]{2,1,0:T(8,128)}, f32[2,256,512]{2,1,0:T(8,128)}, u32[]{:S(2)}, u32[]{:S(2)}) collective-permute-start(f32[2,256,512]{2,1,0:T(8,128)} %trail.21), channel_id=1, source_target_pairs={{0,2},{1,3},{2,0},{3,1},{4,6},{5,7},{6,4},{7,5},{8,10},{9,11},{10,... | collective-permute-start | bytes 3145736 | tf_op jit(solution)/shard_map/ppermute | solution.py:323
  359.6 41.5 %collective-permute-start.66 = (f32[2,256,512]{2,1,0:T(8,128)}, f32[2,256,512]{2,1,0:T(8,128)}, u32[]{:S(2)}, u32[]{:S(2)}) collective-permute-start(f32[2,256,512]{2,1,0:T(8,128)} %trail.19), channel_id=1, source_target_pairs={{0,1},{1,2},{2,3},{3,0},{4,5},{5,6},{6,7},{7,4},{8,9},{9,10},{10,1... | collective-permute-start | bytes 3145736 | tf_op jit(solution)/shard_map/ppermute | solution.py:323
  404.6 21.9 %collective-permute-start.69 = (f32[128,512]{1,0:T(8,128)}, f32[128,512]{1,0:T(8,128)}, u32[]{:S(2)}, u32[]{:S(2)}) collective-permute-start(f32[128,512]{1,0:T(8,128)} %get-tuple-element.81), channel_id=1, source_target_pairs={{0,4},{1,5},{2,6},{3,7},{4,8},{5,9},{6,10},{7,11},{8,12},{9,13},{1... | collective-permute-start | bytes 786440 | tf_op jit(solution)/shard_map/ppermute | solution.py:325
  412.2 96.2 %collective-permute-start.78 = (f32[2,256,512]{2,1,0:T(8,128)}, f32[2,256,512]{2,1,0:T(8,128)}, u32[]{:S(2)}, u32[]{:S(2)}) collective-permute-start(f32[2,256,512]{2,1,0:T(8,128)} %trail.27), channel_id=1, source_target_pairs={{0,4},{1,5},{2,6},{3,7},{4,8},{5,9},{6,10},{7,11},{8,12},{9,13},{1... | collective-permute-start | bytes 3145736 | tf_op jit(solution)/shard_map/ppermute | solution.py:325
  416.9 91.5 %collective-permute-start.79 = (f32[2,256,512]{2,1,0:T(8,128)}, f32[2,256,512]{2,1,0:T(8,128)}, u32[]{:S(2)}, u32[]{:S(2)}) collective-permute-start(f32[2,256,512]{2,1,0:T(8,128)} %trail.29), channel_id=1, source_target_pairs={{0,8},{1,9},{2,10},{3,11},{4,12},{5,13},{6,14},{7,15},{8,0},{9,1},... | collective-permute-start | bytes 3145736 | tf_op jit(solution)/shard_map/ppermute | solution.py:325
  424.6 83.9 %collective-permute-start.80 = (f32[2,256,512]{2,1,0:T(8,128)}, f32[2,256,512]{2,1,0:T(8,128)}, u32[]{:S(2)}, u32[]{:S(2)}) collective-permute-start(f32[2,256,512]{2,1,0:T(8,128)} %trail.31), channel_id=1, source_target_pairs={{0,12},{1,13},{2,14},{3,15},{4,0},{5,1},{6,2},{7,3},{8,4},{9,5},{1... | collective-permute-start | bytes 3145736 | tf_op jit(solution)/shard_map/ppermute | solution.py:325
  426.5 40.4 %collective-permute-start.70 = (f32[128,512]{1,0:T(8,128)S(1)}, f32[128,512]{1,0:T(8,128)}, u32[]{:S(2)}, u32[]{:S(2)}) collective-permute-start(f32[128,512]{1,0:T(8,128)S(1)} %get-tuple-element.82), channel_id=1, source_target_pairs={{0,8},{1,9},{2,10},{3,11},{4,12},{5,13},{6,14},{7,15},{8,0},{9,1},... | collective-permute-start | bytes 786440 | tf_op jit(solution)/shard_map/ppermute | solution.py:325
  426.5 49.4 %collective-permute-start.71 = (f32[128,512]{1,0:T(8,128)S(1)}, f32[128,512]{1,0:T(8,128)}, u32[]{:S(2)}, u32[]{:S(2)}) collective-permute-start(f32[128,512]{1,0:T(8,128)S(1)} %get-tuple-element.83), channel_id=1, source_target_pairs={{0,12},{1,13},{2,14},{3,15},{4,0},{5,1},{6,2},{7,3},{8,4},{9,5},{1... | collective-permute-start | bytes 786440 | tf_op jit(solution)/shard_map/ppermute | solution.py:325
  498.2 107.0 %collective-permute-start.75 = (f32[2,256,512]{2,1,0:T(8,128)}, f32[2,256,512]{2,1,0:T(8,128)}, u32[]{:S(2)}, u32[]{:S(2)}) collective-permute-start(f32[2,256,512]{2,1,0:T(8,128)} %bitcast.103), channel_id=1, source_target_pairs={{0,1},{1,2},{2,3},{3,0},{4,5},{5,6},{6,7},{7,4},{8,9},{9,10},{10,1... | collective-permute-start | bytes 3145736 | tf_op jit(solution)/shard_map/ppermute | solution.py:323
  511.2 23.3 %collective-permute-start.81 = (f32[128,512]{1,0:T(8,128)S(1)}, f32[128,512]{1,0:T(8,128)S(1)}, u32[]{:S(2)}, u32[]{:S(2)}) collective-permute-start(f32[128,512]{1,0:T(8,128)S(1)} %get-tuple-element.85), channel_id=1, source_target_pairs={{0,1},{1,2},{2,3},{3,0},{4,5},{5,6},{6,7},{7,4},{8,9},{9,10},{10,1... | collective-permute-start | bytes 786440 | tf_op jit(solution)/shard_map/ppermute | solution.py:323
  511.2 23.3 %collective-permute-start.82 = (f32[128,512]{1,0:T(8,128)S(1)}, f32[128,512]{1,0:T(8,128)S(1)}, u32[]{:S(2)}, u32[]{:S(2)}) collective-permute-start(f32[128,512]{1,0:T(8,128)S(1)} %get-tuple-element.86), channel_id=1, source_target_pairs={{0,2},{1,3},{2,0},{3,1},{4,6},{5,7},{6,4},{7,5},{8,10},{9,11},{10,... | collective-permute-start | bytes 786440 | tf_op jit(solution)/shard_map/ppermute | solution.py:323
  511.6 22.9 %collective-permute-start.83 = (f32[128,512]{1,0:T(8,128)S(1)}, f32[128,512]{1,0:T(8,128)S(1)}, u32[]{:S(2)}, u32[]{:S(2)}) collective-permute-start(f32[128,512]{1,0:T(8,128)S(1)} %get-tuple-element.87), channel_id=1, source_target_pairs={{0,3},{1,0},{2,1},{3,2},{4,7},{5,4},{6,5},{7,6},{8,11},{9,8},{10,9... | collective-permute-start | bytes 786440 | tf_op jit(solution)/shard_map/ppermute | solution.py:323
  538.2 34.4 %collective-permute-start.84 = (f32[128,512]{1,0:T(8,128)}, f32[128,512]{1,0:T(8,128)S(1)}, u32[]{:S(2)}, u32[]{:S(2)}) collective-permute-start(f32[128,512]{1,0:T(8,128)} %finish.3.a), channel_id=1, source_target_pairs={{0,1},{1,2},{2,3},{3,0},{4,5},{5,6},{6,7},{7,4},{8,9},{9,10},{10,1... | collective-permute-start | bytes 786440 | tf_op jit(solution)/shard_map/ppermute | solution.py:323
  541.9 69.7 %collective-permute-start.76 = (f32[2,256,512]{2,1,0:T(8,128)S(1)}, f32[2,256,512]{2,1,0:T(8,128)}, u32[]{:S(2)}, u32[]{:S(2)}) collective-permute-start(f32[2,256,512]{2,1,0:T(8,128)S(1)} %bitcast.104), channel_id=1, source_target_pairs={{0,2},{1,3},{2,0},{3,1},{4,6},{5,7},{6,4},{7,5},{8,10},{9,11},{10,... | collective-permute-start | bytes 3145736 | tf_op jit(solution)/shard_map/ppermute | solution.py:323
  541.9 71.1 %collective-permute-start.77 = (f32[2,256,512]{2,1,0:T(8,128)S(1)}, f32[2,256,512]{2,1,0:T(8,128)}, u32[]{:S(2)}, u32[]{:S(2)}) collective-permute-start(f32[2,256,512]{2,1,0:T(8,128)S(1)} %bitcast.105), channel_id=1, source_target_pairs={{0,3},{1,0},{2,1},{3,2},{4,7},{5,4},{6,5},{7,6},{8,11},{9,8},{10,9... | collective-permute-start | bytes 3145736 | tf_op jit(solution)/shard_map/ppermute | solution.py:323
  542.8 51.8 %collective-permute-start.85 = (f32[128,512]{1,0:T(8,128)}, f32[128,512]{1,0:T(8,128)S(1)}, u32[]{:S(2)}, u32[]{:S(2)}) collective-permute-start(f32[128,512]{1,0:T(8,128)} %finish.3.a), channel_id=1, source_target_pairs={{0,2},{1,3},{2,0},{3,1},{4,6},{5,7},{6,4},{7,5},{8,10},{9,11},{10,... | collective-permute-start | bytes 786440 | tf_op jit(solution)/shard_map/ppermute | solution.py:323
  572.7 24.6 %collective-permute-start.86 = (f32[128,512]{1,0:T(8,128)}, f32[128,512]{1,0:T(8,128)S(1)}, u32[]{:S(2)}, u32[]{:S(2)}) collective-permute-start(f32[128,512]{1,0:T(8,128)} %finish.3.a), channel_id=1, source_target_pairs={{0,3},{1,0},{2,1},{3,2},{4,7},{5,4},{6,5},{7,6},{8,11},{9,8},{10,9... | collective-permute-start | bytes 786440 | tf_op jit(solution)/shard_map/ppermute | solution.py:323
  600.3 26.6 %collective-permute-start.87 = (f32[2,256,512]{2,1,0:T(8,128)}, f32[2,256,512]{2,1,0:T(8,128)}, u32[]{:S(2)}, u32[]{:S(2)}) collective-permute-start(f32[2,256,512]{2,1,0:T(8,128)} %bitcast.107), channel_id=1, source_target_pairs={{0,4},{1,5},{2,6},{3,7},{4,8},{5,9},{6,10},{7,11},{8,12},{9,13},{1... | collective-permute-start | bytes 3145736 | tf_op jit(solution)/shard_map/ppermute | solution.py:325
  600.3 50.7 %collective-permute-start.88 = (f32[2,256,512]{2,1,0:T(8,128)}, f32[2,256,512]{2,1,0:T(8,128)}, u32[]{:S(2)}, u32[]{:S(2)}) collective-permute-start(f32[2,256,512]{2,1,0:T(8,128)} %bitcast.108), channel_id=1, source_target_pairs={{0,8},{1,9},{2,10},{3,11},{4,12},{5,13},{6,14},{7,15},{8,0},{9,1},... | collective-permute-start | bytes 3145736 | tf_op jit(solution)/shard_map/ppermute | solution.py:325
  605.2 47.1 %collective-permute-start.89 = (f32[2,256,512]{2,1,0:T(8,128)}, f32[2,256,512]{2,1,0:T(8,128)S(1)}, u32[]{:S(2)}, u32[]{:S(2)}) collective-permute-start(f32[2,256,512]{2,1,0:T(8,128)} %bitcast.109), channel_id=1, source_target_pairs={{0,12},{1,13},{2,14},{3,15},{4,0},{5,1},{6,2},{7,3},{8,4},{9,5},{1... | collective-permute-start | bytes 3145736 | tf_op jit(solution)/shard_map/ppermute | solution.py:325
  (124 other events, 879.6 us)

commit v2 on v0

v2 whole, which is shorter than its diff:
```python
import functools

import jax
import jax.numpy as jnp
from jax import lax
from jax.experimental import pallas as pl
from jax.experimental.pallas import tpu as pltpu
from jax.sharding import PartitionSpec as P

F32 = jnp.float32
BF16 = jnp.bfloat16
STEPS = 6
V, H, S = (pl.BlockSpec(memory_space=m) for m in (pltpu.VMEM, pltpu.HBM, pltpu.SMEM))


def split(value):
    high = value.astype(BF16)
    return high, (value - high.astype(F32)).astype(BF16)


def dot(a, b):
    return jnp.dot(a, b, preferred_element_type=F32)


def call(kernel, name, mib, inputs, outputs, scratch=()):
    specs, operands = zip(*inputs)
    return pl.pallas_call(
        kernel,
        in_specs=specs,
        out_specs=[V] * len(outputs),
        out_shape=[jax.ShapeDtypeStruct(*o) for o in outputs],
        scratch_shapes=scratch,
        compiler_params=pltpu.CompilerParams(vmem_limit_bytes=mib << 20),
        name=name,
    )(*operands)


def fetch(pairs, sems):
    copies = [pltpu.make_async_copy(a, b, sems.at[i]) for i, (a, b) in enumerate(pairs)]
    for copy in copies:
        copy.start()
    return copies


def gram_kernel(blocks, s, meta, scale, inverse, rhs, tiles, _, __, keep, send, d_buf, r_buf, t_buf, product, sems):
    x, u, z = meta[0], meta[2], meta[3]
    group = pl.ds(pl.multiple_of(z * 128, 128), 128)
    copies = fetch(
        [(tiles.at[s, pl.ds(0, s)], t_buf)]
        + [(inverse.at[b], d_buf.at[i]) for i, b in enumerate(blocks)]
        + [(rhs.at[b, :, group], r_buf.at[i]) for i, b in enumerate(blocks)],
        sems,
    )
    for copy in copies:
        copy.wait()

    def store(slot, row, ey, at):
        row = row + ey * 32
        keep[ey, at] = product[slot, pl.ds(pl.multiple_of(row + u * 16, 16), 16), :]
        send[ey, at] = product[slot, pl.ds(pl.multiple_of(row + (1 - u) * 16, 16), 16), :]

    base = 4 * len(blocks)
    for j in range(s):
        slot = j % 2
        product[slot] = dot(d_buf[len(blocks) - 1], t_buf[j]) * scale[s, j]
        for zz in range(4):
            for ex in range(4):
                row = (zz * 4 + lax.rem(x + ex, 4)) * 128
                for ey in range(4):
                    store(slot, row, ey, base + 16 * j + ex * 4 + zz)
    slot = s % 2
    for i in range(len(blocks)):
        high, low = split(r_buf[i])
        both = jnp.concatenate([high, low], axis=0)
        for dz in range(4):
            chunk = lax.rem(z + 4 - dz, 4) * 4 + x
            rows = d_buf[i, pl.ds(pl.multiple_of(chunk * 128, 128), 128), :]
            row = (i * 4 + dz) * 128
            product[slot, pl.ds(row, 128), :] = dot(jnp.concatenate([rows, rows], axis=1), both)
            for ey in range(4):
                store(slot, row, ey, i * 4 + dz)


def gram(blocks, s, meta, scale, inverse, rhs, tiles, *after):
    out = ((4, 4 * len(blocks) + 16 * s, 16, 128), F32)
    n = len(blocks)
    return call(
        functools.partial(gram_kernel, blocks, s),
        "gram",
        58 if s == 1 else 32,
        [(S, meta), (S, scale), (H, inverse), (H, rhs), (H, tiles)] + [(H, a) for a in after],
        [out, out],
        [
            pltpu.VMEM((n, 2048, 256), BF16),
            pltpu.VMEM((n, 256, 128), F32),
            pltpu.VMEM((s, 256, 128), BF16),
            pltpu.VMEM((2, 2048, 128), F32),
            pltpu.SemaphoreType.DMA((1 + 2 * n,)),
        ],
    )


def step_kernel(count, meta, *refs):
    y, u, z = meta[1], meta[2], meta[3]
    pieces, refs = refs[:4], refs[4:]
    older, refs = refs[: count - 1], refs[count - 1 :]
    gathered = len(refs) == 8
    gram_refs, refs = refs[:-7], refs[-7:]
    chunks, solved, g_buf, sems = refs[:4], refs[4], refs[5], refs[6]
    sources = [gram_refs[0].at[lax.rem(z + 4 - d, 4)] if gathered else gram_refs[d] for d in range(4)]
    copies = fetch([(sources[d], g_buf.at[d]) for d in range(4)], sems)
    for ey in range(4):
        row = lax.rem(y + 4 - ey, 4) * 32
        for eu in range(2):
            at = pl.multiple_of(row + (u + eu - 2 * u * eu) * 16, 16)
            for dz in range(4):
                solved[dz, pl.ds(at, 16), :] = pieces[ey][eu, dz]
    for copy in copies:
        copy.wait()
    total = jnp.zeros((256, 128), F32)
    for j in range(count):
        block = jnp.concatenate([g_buf[d, pl.ds(16 * j, 16)].reshape(256, 128) for d in range(4)], axis=1)
        source = solved if j == count - 1 else older[j]
        a_high, a_low = split(block)
        b_high, b_low = split(source[...].reshape(512, 128))
        total = total + (dot(a_high, b_high) + (dot(a_high, b_low) + dot(a_low, b_high)))
    total = total.reshape(4, 4, 16, 128)
    for ex in range(4):
        for zz in range(4):
            chunks[ex][lax.rem(z + 4 - zz, 4)] = total[ex, zz]


def step(meta, pieces, older, pieces_z):
    count = len(older) + 1
    *chunks, solved = call(
        functools.partial(step_kernel, count),
        "step",
        24,
        [(S, meta)] + [(V, p) for p in pieces] + [(V, o) for o in older] + [(H, g) for g in pieces_z],
        [((4, 16, 128), F32)] * 4 + [((4, 128, 128), F32)],
        [pltpu.VMEM((4, 16 * count, 16, 128), F32), pltpu.SemaphoreType.DMA((4,))],
    )
    return chunks, solved


def early_kernel(meta, *refs):
    z = meta[3]
    own, others, solved, both = refs[:5], refs[5:8], refs[8], refs[9]
    for k in range(5):
        for d in range(4):
            at = pl.multiple_of(lax.rem(z + 4 - d, 4) * 128, 128)
            value = own[k][0] if d == 0 else others[d - 1][k]
            high, low = split(value)
            solved[k, :, pl.ds(at, 128)] = value
            both[k, pl.ds(0, 128), pl.ds(at, 128)] = high
            both[k, pl.ds(128, 128), pl.ds(at, 128)] = low


def early(meta, own, others):
    return call(
        early_kernel,
        "early",
        16,
        [(S, meta)] + [(V, o) for o in own] + [(V, o) for o in others],
        [((5, 128, 512), F32), ((5, 256, 512), BF16)],
    )


def late_kernel(meta, a, b, c, d, solved, both):
    y, u, z = meta[1], meta[2], meta[3]
    for ey, piece in enumerate((a, b, c, d)):
        row = lax.rem(y + 4 - ey, 4) * 32
        for eu in range(2):
            at = pl.multiple_of(row + (u + eu - 2 * u * eu) * 16, 16)
            low_at = pl.multiple_of(at + 128, 16)
            for dz in range(4):
                group = pl.ds(pl.multiple_of(lax.rem(z + 4 - dz, 4) * 128, 128), 128)
                value = piece[eu, dz]
                high, low = split(value)
                solved[0, pl.ds(at, 16), group] = value
                both[0, pl.ds(at, 16), group] = high
                both[0, pl.ds(low_at, 16), group] = low


def late(meta, pieces):
    return call(
        late_kernel,
        "late",
        8,
        [(S, meta)] + [(V, p) for p in pieces],
        [((1, 128, 512), F32), ((1, 256, 512), BF16)],
    )


def trail_kernel(count, first, scale, tiles, early_both, late_both, _, *refs):
    outs, t_buf, sems = refs[:count], refs[count], refs[count + 1]
    copies = fetch([(tiles.at[first[i]], t_buf.at[i]) for i in range(count)], sems)
    for i in range(count):
        copies[i].wait()
        total = None
        for k in range(STEPS):
            own = t_buf[i, k]
            value = early_both[k] if k < 5 else late_both[0]
            part = dot(jnp.concatenate([own, own], axis=1), value) * scale[first[i], k]
            total = part if total is None else total + part
        outs[i][...] = total


def trail(first, scale, tiles, early_both, late_both, after):
    count = first.shape[0]
    return call(
        functools.partial(trail_kernel, count),
        "trail",
        56,
        [(S, first), (S, scale), (H, tiles), (V, early_both), (V, late_both), (H, after)],
        [((256, 512), F32)] * count,
        [pltpu.VMEM((count, 6, 256, 128), BF16), pltpu.SemaphoreType.DMA((count,))],
    )


def sum_sub_kernel(me, a0, a1, b0, b1, c0, c1, *outs):
    for e in range(4):
        at = lax.rem(me[0] + e, 4)
        rows = pl.ds(pl.multiple_of(lax.rem(at, 2) * 128, 128), 128)

        @pl.when(at < 2)
        def _():
            outs[e][...] = a0[rows, :] + (b0[rows, :] + c0[rows, :])

        @pl.when(at >= 2)
        def _():
            outs[e][...] = a1[rows, :] + (b1[rows, :] + c1[rows, :])


def sum_sub(me, parts):
    return call(sum_sub_kernel, "sum_sub", 24, [(S, me)] + [(V, p) for p in parts], [((128, 512), F32)] * 4)


def finish_kernel(at, rhs, a, b, c, out, buf, sem):
    copy = pltpu.make_async_copy(rhs.at[at[0], pl.ds(pl.multiple_of(at[1] * 128, 128), 128)], buf, sem)
    copy.start()
    total = a[...] + (b[...] + c[...])
    copy.wait()
    out[...] = buf[...] - total


def finish(at, rhs, parts):
    return call(
        finish_kernel,
        "finish",
        56,
        [(S, at), (H, rhs)] + [(V, p) for p in parts],
        [((128, 512), F32)],
        [pltpu.VMEM((128, 512), F32), pltpu.SemaphoreType.DMA],
    )[0]


def place_kernel(me, own, back, ahead, low, high, out0, out1):
    def put(at, rows, value):
        start = pl.ds(pl.multiple_of(lax.rem(at, 2) * 128 + rows, 64), value.shape[0])

        @pl.when(at < 2)
        def _():
            out0[start, :] = value

        @pl.when(at >= 2)
        def _():
            out1[start, :] = value

    for e, ref in ((0, own), (3, back), (1, ahead)):
        put(lax.rem(me[0] + e, 4), 0, ref[...])
    put(lax.rem(me[0] + 2, 4), 0, low[...])
    put(lax.rem(me[0] + 2, 4), 64, high[...])


def place(me, parts):
    return call(place_kernel, "place", 16, [(S, me)] + [(V, p) for p in parts], [((256, 512), F32)] * 2)


def on_device(rhs_blocks, factor_tiles, tile_scale, diag_inverse):
    row, column = lax.axis_index("prow"), lax.axis_index("pcol")
    y, u, z, x = row // 2, row % 2, column // 4, column % 4
    meta = jnp.stack([x, y, u, z]).astype(jnp.int32)
    tiles = jnp.transpose(factor_tiles, (0, 2, 1, 3))

    def shift(value, axis, d):
        if axis == "x":
            return lax.ppermute(value, "pcol", [(i, i // 4 * 4 + (i + d) % 4) for i in range(16)])
        if axis == "z":
            return lax.ppermute(value, "pcol", [(i, (i + 4 * d) % 16) for i in range(16)])
        if axis == "y":
            return lax.ppermute(value, "prow", [(i, (i + 2 * d) % 8) for i in range(8)])
        return lax.ppermute(value, "prow", [(i, i ^ 1) for i in range(8)])

    def exchange(values, axis):
        return [values[0]] + [shift(values[d], axis, d) for d in (1, 2, 3)]

    def spread(value, axis):
        return exchange([value] * 4, axis)

    def reduce_rows(keep, send):
        half = keep + shift(send, "core", 1)
        groups = [[2 * i + core for i in range(4)] for core in range(2)]
        parts = lax.all_to_all(half, "prow", 0, 0, axis_index_groups=groups)
        return half, (parts[0] + parts[1]) + (parts[2] + parts[3])

    def gather_z(value):
        groups = [[4 * i + j for i in range(4)] for j in range(4)]
        return [lax.all_gather(value, "pcol", axis_index_groups=groups)]

    def gather(piece):
        both = jnp.stack([piece, shift(piece, "core", 1)])
        return both, spread(both, "y")

    start, grams = [], {}

    def make(s, *after):
        blocks = (0, 1) if s == 1 else (s,)
        half, total = reduce_rows(*gram(blocks, s, meta, tile_scale, diag_inverse, rhs_blocks, tiles, *after))
        start.extend(total[4 * i : 4 * i + 4] for i in range(len(blocks)))
        block = total[4 * len(blocks) :]
        grams[s] = spread(block, "z") if s < 3 else gather_z(block)
        return half

    half = make(2, make(1, meta, meta), meta)
    solved = []
    piece = start[0]
    for s in range(1, STEPS):
        both, pieces = gather(piece)
        if s == 1:
            half = make(3, half, both)
        chunks, latest = step(meta, pieces, solved, grams[s])
        if s < 3:
            half = make(s + 3, half, chunks[0])
        solved.append(latest)
        a, b, c, d = exchange(chunks, "x")
        piece = start[s] - ((a + b) + (c + d))

    others = exchange([jnp.stack([v[-d % 4] for v in solved]) for d in range(4)], "z")[1:]
    solved_early, both_early = early(meta, solved, others)
    piece = jnp.stack(exchange([piece[-d % 4] for d in range(4)], "z"))
    solved_late, both_late = late(meta, gather(piece)[1])

    axes = (("x", "z", x, z, 6), ("z", "x", z, x, 14))

    def chunks_of(offsets, after):
        first = jnp.stack([base + 2 * ((me + d) % 4) + i for d in offsets for _, _, me, _, base in axes for i in range(2)])
        return trail(first.astype(jnp.int32), tile_scale, tiles, both_early, both_late, after)

    def ring(values):
        return [(shift(up, axis, 1), shift(down, axis, 3)) for axis, up, down in values]

    one, two = [a[0] for a in axes], [a[1] for a in axes]
    far = chunks_of((2,), meta)
    moved = ring([(one[h], far[2 * h], far[2 * h + 1]) for h in range(2)])
    near = chunks_of((1, 3), far[0])
    own = chunks_of((0,), near[0])
    ups = [jnp.stack([near[2 * h] + moved[h][0], near[2 * h + 1]]) for h in range(2)]
    downs = [jnp.stack([near[4 + 2 * h], near[5 + 2 * h] + moved[h][1]]) for h in range(2)]
    moved = ring([(one[h], ups[h], downs[h]) for h in range(2)])
    subs = []
    for h in range(2):
        other = axes[h][3].astype(jnp.int32)[None]
        below, above = moved[h]
        subs.append(sum_sub(other, (own[2 * h], own[2 * h + 1], below[0], below[1], above[0], above[1])))
    moved = ring([(two[h], subs[h][2][:64], subs[h][2][64:]) for h in range(2)])
    ups = [subs[h][1].at[:64].add(moved[h][0]) for h in range(2)]
    downs = [subs[h][3].at[64:].add(moved[h][1]) for h in range(2)]
    moved = ring([(two[h], ups[h], downs[h]) for h in range(2)])
    done = []
    for h, (_, _, me, other, base) in enumerate(axes):
        at = jnp.stack([base + 2 * me + other // 2, other % 2]).astype(jnp.int32)
        done.append(finish(at, rhs_blocks, (subs[h][0],) + moved[h]))
    near = ring([(two[h], done[h], done[h]) for h in range(2)])
    far = ring([(two[h], near[h][0][:64], near[h][1][64:]) for h in range(2)])
    own = []
    for h in range(2):
        other = axes[h][3].astype(jnp.int32)[None]
        own.append(jnp.stack(place(other, (done[h],) + near[h] + far[h])))
    near = ring([(one[h], own[h], own[h]) for h in range(2)])
    far = ring([(one[h], near[h][0][0], near[h][1][1]) for h in range(2)])
    trailing = jnp.zeros((16, 256, 512), F32)
    for h, (_, _, me, _, base) in enumerate(axes):
        base = base - 6
        far_chunk = base + 2 * ((me + 2) % 4)
        trailing = lax.dynamic_update_slice(trailing, own[h], (base + 2 * me, 0, 0))
        trailing = lax.dynamic_update_slice(trailing, near[h][0], (base + 2 * ((me + 3) % 4), 0, 0))
        trailing = lax.dynamic_update_slice(trailing, near[h][1], (base + 2 * ((me + 1) % 4), 0, 0))
        trailing = lax.dynamic_update_slice(trailing, far[h][0][None], (far_chunk, 0, 0))
        trailing = lax.dynamic_update_slice(trailing, far[h][1][None], (far_chunk + 1, 0, 0))
    return jnp.concatenate([solved_early, solved_late]), trailing


def solution(mesh):
    in_specs = (P(None, "prow", None), P(None, "prow", None, "pcol"), P(), P(None, None, "prow"))
    out_specs = (P(None, "pcol", None), P(None, "prow", None))
    return jax.shard_map(
        on_device, mesh=mesh, in_specs=in_specs, out_specs=out_specs, check_vma=False
    )
```

time: 1090 us -> 537 us (0.49)
  waiting for transfers between devices: 920 us -> 168 us
  starting transfers between devices: 1.13 us -> 131 us
  matrix products: 89.5 us -> 0 us
  blocking collectives: 0 us -> 66.8 us
  Pallas kernels: 0 us -> 60.3 us
  local copies, waits for them, and re-layouts: 31.6 us -> 57.2 us
    psum x12 -> x0, waiting for transfers between devices: 920 us -> none  [the longest x5 420 us: on_device(): remainder = rhs_blocks[column] - lax.psum(partial_value[column], 'pcol')]
    ppermute x0 -> x88, waiting for transfers between devices: none -> 150 us  [the longest x31 66 us: shift(): lax.ppermute(value, 'pcol', [(i, i // 4 * 4 + (i + d) % 4) for i in range...]
    ppermute x0 -> x88, starting transfers between devices: none -> 118 us  [the longest x28 50 us: shift(): lax.ppermute(value, 'pcol', [(i, (i + 4 * d) % 16) for i in range(16)])]
    dot_general x12 -> x0, matrix products: 89.5 us -> none  [the longest x6 76 us: on_device(): jnp.einsum('sqj,jr->sqr', scaled_tiles, solved_rows, precision=lax.Precis...]
    all_to_all x0 -> x2, blocking collectives: none -> 66.8 us  [reduce_rows(): parts = lax.all_to_all(half, 'prow', 0, 0, axis_index_groups=groups)]
    pallas_call x0 -> x21, Pallas kernels: none -> 60.3 us  [call(): pl.pallas_call(kernel, in_specs=specs, out_specs=[V] * len(outputs), out_...]
    all_to_all x0 -> x3, waiting for transfers between devices: none -> 17.4 us  [reduce_rows(): parts = lax.all_to_all(half, 'prow', 0, 0, axis_index_groups=groups)]
    unnamed x31 -> x101, local copies, waits for them, and re-layouts: 22.9 us -> 37.8 us
  transfers between devices with their start and end apart: 12 -> 94, of which waited for: 12 -> 54; matrix products, arithmetic and copies ran while one was open for 0% -> 8% of each run, Pallas kernels for 0% -> 8%
where the time goes in v2:
time: 537 us; the launch traced here: 527 us
  waiting for transfers between devices  168 us (31%)
  starting transfers between devices  131 us (24%)
  blocking collectives  66.8 us (12%)
  Pallas kernels  60.3 us (11%)
  local copies, waits for them, and re-layouts  57.2 us (11%)
  other arithmetic  28.3 us (5%)
  between operations  15.3 us (3%)
    all_to_all x2, blocking collectives, reduce_rows(): parts = lax.all_to_all(half, 'prow', 0, 0, axis_index_groups=groups)  66.8 us
    ppermute x31, waiting for transfers between devices, shift(): lax.ppermute(value, 'pcol', [(i, i // 4 * 4 + (i + d) % 4) for i in range...  66 us
    pallas_call x21, Pallas kernels, call(): pl.pallas_call(kernel, in_specs=specs, out_specs=[V] * len(outputs), out_...  60.3 us
    ppermute x28, starting transfers between devices, shift(): lax.ppermute(value, 'pcol', [(i, (i + 4 * d) % 16) for i in range(16)])  50 us
    ppermute x31, starting transfers between devices, shift(): lax.ppermute(value, 'pcol', [(i, i // 4 * 4 + (i + d) % 4) for i in range...  42.8 us
    ppermute x18, waiting for transfers between devices, shift(): return lax.ppermute(value, 'prow', [(i, (i + 2 * d) % 8) for i in range(8)])  41 us
    unnamed x101, local copies, waits for them, and re-layouts  37.8 us
    ppermute x28, waiting for transfers between devices, shift(): lax.ppermute(value, 'pcol', [(i, (i + 4 * d) % 16) for i in range(16)])  34.8 us
  transfers between devices with their start and end apart: 94, of which 54 were waited for; matrix products, arithmetic and copies ran while one was open for 8% of the time, Pallas kernels for 8%

profile of v2, /device:TPU:6, one launch (start us, length us, event | category | flops | bytes accessed | tf_op | source)
XLA Modules:
  0.0 527.1 jit_solution(6670102453982488438)
XLA Ops:
  9.2 4.7 gram.5
  18.5 4.5 all-to-all-start
  23.0 3.5 copy-done
  29.2 3.0 gram.6
  32.3 3.3 all-to-all-done
  39.4 3.5 copy-done.1
  45.6 4.7 gram.7
  50.6 4.3 all-to-all-start.1
  61.5 3.6 collective-permute-start.6
  65.1 8.3 %collective-permute-done.2.refs_1_ = f32[2,4,16,128]{3,2,1,0:T(8,128)S(1)} collective-permute-done((f32[2,4,16,128]{3,2,1,0:T(8,128)S(1)}, f32[2,4,16,128]{3,2,1,0:T(8,128)S(1)}, u32[]{:S(2)}, u32[]{:S(2)}) %collective-permute-start.2) | collective-permute-done | bytes 65568 | tf_op jit(solution)/shard_map/ppermute | solution.py:292
  73.4 4.0 collective-permute-start.7
  78.7 3.0 collective-permute-done.4.refs_3_
  86.4 3.5 copy-done.2
  92.6 5.0 gram.8
  99.0 4.4 all-to-all-start.2
  104.9 3.2 collective-permute-start.8
  112.4 14.1 %all-to-all-done.2 = f32[4,52,16,128]{3,2,1,0:T(8,128)} async-done(((f32[4,52,16,128]{3,2,1,0:T(8,128)}), f32[4,52,16,128]{3,2,1,0:T(8,128)}, u32[]{:S(2)}, u32[]{:S(2)}) %all-to-all-start.2) | async-done | bytes 1703968 | tf_op jit(solution)/shard_map/all_to_all | solution.py:304
  130.2 3.3 collective-permute-start.17
  134.8 4.9 collective-permute-done.12.refs_1_
  139.7 5.8 %collective-permute-done.13.refs_2_ = f32[2,4,16,128]{3,2,1,0:T(8,128)S(1)} collective-permute-done((f32[2,4,16,128]{3,2,1,0:T(8,128)S(1)}, f32[2,4,16,128]{3,2,1,0:T(8,128)S(1)}, u32[]{:S(2)}, u32[]{:S(2)}) %collective-permute-start.13) | collective-permute-done | bytes 65568 | tf_op jit(solution)/shard_map/ppermute | solution.py:292
  145.5 4.3 collective-permute-done.14.refs_3_
  156.8 3.4 copy-done.3
  160.3 5.7 %gram.9 = (f32[4,84,16,128]{3,2,1,0:T(8,128)S(1)}, f32[4,84,16,128]{3,2,1,0:T(8,128)}) custom-call(s32[4]{0:T(128)S(1)} %copy-done.27, f32[22,6]{1,0:T(8,128)S(1)} %copy-done.16, bf16[6,2048,256]{2,1,0:T(8,128)(2,1)S(1)} %bitcast.129, f32[22,256,512]{2,1,0:T(8,128)} %rhs.17, bf16[22,6,256,128]{3,2,1,0:T(8,128)(2,1)S(1)} %bitcast.127, ...), custom_call_target="tpu_custom_call" | custom-call | tf_op jit(solution)/shard_map/gram/pallas_call | solution.py:27
  166.0 31.1 %all_to_all.25 = f32[4,68,16,128]{3,2,1,0:T(8,128)S(1)} all-to-all(f32[4,68,16,128]{3,2,1,0:T(8,128)S(1)} %add.414._), channel_id=1, replica_groups={{0,32,64,96},{16,48,80,112},{1,33,65,97},{17,49,81,113},{2,34,66,98},{1..., dimensions={0} | all-to-all | bytes 4456448 | tf_op jit(solution)/shard_map/all_to_all | solution.py:304
  201.2 35.7 %all_to_all.26 = f32[4,84,16,128]{3,2,1,0:T(8,128)S(1)} all-to-all(f32[4,84,16,128]{3,2,1,0:T(8,128)S(1)} %add.421), channel_id=1, replica_groups={{0,32,64,96},{16,48,80,112},{1,33,65,97},{17,49,81,113},{2,34,66,98},{1..., dimensions={0} | all-to-all | bytes 5505024 | tf_op jit(solution)/shard_map/all_to_all | solution.py:304
  239.4 3.2 collective-permute-start.19
  250.1 3.3 collective-permute-done.23.refs_1_
  291.6 3.0 collective-permute-done.39.refs_1_
  318.8 3.1 collective-permute-start.54
  332.9 5.5 %trail.3 = (f32[256,512]{1,0:T(8,128)}, f32[256,512]{1,0:T(8,128)}, f32[256,512]{1,0:T(8,128)}, f32[256,512]{1,0:T(8,128)}) custom-call(s32[4]{0:T(128)} %get-tuple-element.224.first, f32[22,6]{1,0:T(8,128)} %copy.14.scale, bf16[22,6,256,128]{3,2,1,0:T(8,128)(2,1)} %bitcast.121, bf16[5,256,512]{2,1,0:T(8,128)(2,1)} %copy-done.7, ...), custom_call_target="tpu_custom_call" | custom-call | tf_op jit(solution)/shard_map/trail/pallas_call | solution.py:27
  341.5 8.6 %trail.4 = (f32[256,512]{1,0:T(8,128)}, f32[256,512]{1,0:T(8,128)}, f32[256,512]{1,0:T(8,128)}, f32[256,512]{1,0:T(8,128)}, f32[256,512]{1,0:T(8,128)}, /*index=...) custom-call(s32[8]{0:T(128)} %stack.262.first, f32[22,6]{1,0:T(8,128)} %copy.14.scale, ...), custom_call_target="tpu_custom_call" | custom-call | tf_op jit(solution)/shard_map/trail/pallas_call | solution.py:27
  350.3 3.2 collective-permute-start.74
  353.5 5.6 %trail.5 = (f32[256,512]{1,0:T(8,128)}, f32[256,512]{1,0:T(8,128)}, f32[256,512]{1,0:T(8,128)}, f32[256,512]{1,0:T(8,128)}) custom-call(s32[4]{0:T(128)} %get-tuple-element.223.first, f32[22,6]{1,0:T(8,128)} %copy.14.scale, bf16[22,6,256,128]{3,2,1,0:T(8,128)(2,1)} %bitcast.123, bf16[5,256,512]{2,1,0:T(8,128)(2,1)} %copy-done.7, ...), custom_call_target="tpu_custom_call" | custom-call | tf_op jit(solution)/shard_map/trail/pallas_call | solution.py:27
  359.3 3.3 collective-permute-start.57
  366.8 3.2 collective-permute-start.75
  370.0 12.2 %collective-permute-done.57 = f32[2,256,512]{2,1,0:T(8,128)S(1)} collective-permute-done((f32[2,256,512]{2,1,0:T(8,128)S(1)}, f32[2,256,512]{2,1,0:T(8,128)S(1)}, u32[]{:S(2)}, u32[]{:S(2)}) %collective-permute-start.57) | collective-permute-done | bytes 1048608 | tf_op jit(solution)/shard_map/ppermute | solution.py:288
  382.3 3.8 collective-permute-done.59
  388.0 3.2 collective-permute-start.62
  393.7 3.7 collective-permute-start.63
  405.1 3.8 collective-permute-start.65
  409.2 5.5 %collective-permute-done.64.back = f32[128,512]{1,0:T(8,128)S(1)} collective-permute-done((f32[128,512]{1,0:T(8,128)}, f32[128,512]{1,0:T(8,128)S(1)}, u32[]{:S(2)}, u32[]{:S(2)}) %collective-permute-start.64) | collective-permute-done | bytes 262176 | tf_op jit(solution)/shard_map/ppermute | solution.py:290
  414.9 3.3 collective-permute-start.67
  428.7 20.4 %collective-permute-done.77.b = f32[128,512]{1,0:T(8,128)S(1)} collective-permute-done((f32[128,512]{1,0:T(8,128)S(1)}, f32[128,512]{1,0:T(8,128)S(1)}, u32[]{:S(2)}, u32[]{:S(2)}) %collective-permute-start.77) | collective-permute-done | bytes 262176 | tf_op jit(solution)/shard_map/ppermute | solution.py:288
  457.0 4.6 collective-permute-done.80.back
  463.7 4.3 collective-permute-done.82.low
  486.2 3.2 collective-permute-start.85
  490.7 17.3 %collective-permute-done.84 = f32[2,256,512]{2,1,0:T(8,128)S(1)} collective-permute-done((f32[2,256,512]{2,1,0:T(8,128)}, f32[2,256,512]{2,1,0:T(8,128)S(1)}, u32[]{:S(2)}, u32[]{:S(2)}) %collective-permute-start.84) | collective-permute-done | bytes 1048608 | tf_op jit(solution)/shard_map/ppermute | solution.py:290
  509.2 3.3 collective-permute-start.87
  (341 shorter events, 206.6 us)
Async XLA Ops:
  18.5 17.0 %all-to-all-start = ((f32[4,24,16,128]{3,2,1,0:T(8,128)}), f32[4,24,16,128]{3,2,1,0:T(8,128)S(1)}, u32[]{:S(2)}, u32[]{:S(2)}) async-start(f32[4,24,16,128]{3,2,1,0:T(8,128)} %add.393._), calls=%async_computation | async-start | bytes 1572864 | tf_op jit(solution)/shard_map/all_to_all | solution.py:304
  50.3 33.1 %collective-permute-start.26 = (f32[4,52,16,128]{3,2,1,0:T(8,128)}, f32[4,52,16,128]{3,2,1,0:T(8,128)}, u32[]{:S(2)}, u32[]{:S(2)}) collective-permute-start(f32[4,52,16,128]{3,2,1,0:T(8,128)} %get-tuple-element.132), channel_id=1, source_target_pairs={{0,16},{16,0},{32,48},{48,32},{64,80},{80,64},{96,112},{112,96},{1... | collective-permute-start | bytes 5111816 | tf_op jit(solution)/shard_map/ppermute | solution.py:293
  50.6 48.4 %all-to-all-start.1 = ((f32[4,36,16,128]{3,2,1,0:T(8,128)}), f32[4,36,16,128]{3,2,1,0:T(8,128)}, u32[]{:S(2)}, u32[]{:S(2)}) async-start(f32[4,36,16,128]{3,2,1,0:T(8,128)} %add.400._), calls=%async_computation.1 | async-start | bytes 2359296 | tf_op jit(solution)/shard_map/all_to_all | solution.py:304
  54.9 18.6 %collective-permute-start.2 = (f32[2,4,16,128]{3,2,1,0:T(8,128)S(1)}, f32[2,4,16,128]{3,2,1,0:T(8,128)S(1)}, u32[]{:S(2)}, u32[]{:S(2)}) collective-permute-start(f32[2,4,16,128]{3,2,1,0:T(8,128)S(1)} %pad_maximum_fusion.7.refs_0_.__), channel_id=1, source_target_pairs={{0,32},{16,48},{32,64},{48,80},{64,96},{80,112},{96,0},{112,16},{1... | collective-permute-start | bytes 196616 | tf_op jit(solution)/shard_map/ppermute | solution.py:292
  56.9 20.6 %collective-permute-start.3 = (f32[2,4,16,128]{3,2,1,0:T(8,128)S(1)}, f32[2,4,16,128]{3,2,1,0:T(8,128)S(1)}, u32[]{:S(2)}, u32[]{:S(2)}) collective-permute-start(f32[2,4,16,128]{3,2,1,0:T(8,128)S(1)} %pad_maximum_fusion.7.refs_0_.__), channel_id=1, source_target_pairs={{0,64},{16,80},{32,96},{48,112},{64,0},{80,16},{96,32},{112,48},{1... | collective-permute-start | bytes 196616 | tf_op jit(solution)/shard_map/ppermute | solution.py:292
  59.6 22.1 %collective-permute-start.5 = (f32[16,16,128]{2,1,0:T(8,128)S(1)}, f32[16,16,128]{2,1,0:T(8,128)S(1)}, u32[]{:S(2)}, u32[]{:S(2)}) collective-permute-start(f32[16,16,128]{2,1,0:T(8,128)S(1)} %slice_bitcast_fusion.13.refs_4_), channel_id=1, source_target_pairs={{0,4},{1,5},{2,6},{3,7},{4,8},{5,9},{6,10},{7,11},{8,12},{9,13},{1... | collective-permute-start | bytes 393224 | tf_op jit(solution)/shard_map/ppermute | solution.py:290
  61.5 20.2 %collective-permute-start.6 = (f32[16,16,128]{2,1,0:T(8,128)S(1)}, f32[16,16,128]{2,1,0:T(8,128)S(1)}, u32[]{:S(2)}, u32[]{:S(2)}) collective-permute-start(f32[16,16,128]{2,1,0:T(8,128)S(1)} %slice_bitcast_fusion.13.refs_4_), channel_id=1, source_target_pairs={{0,8},{1,9},{2,10},{3,11},{4,12},{5,13},{6,14},{7,15},{8,0},{9,1},... | collective-permute-start | bytes 393224 | tf_op jit(solution)/shard_map/ppermute | solution.py:290
  73.4 8.3 %collective-permute-start.7 = (f32[16,16,128]{2,1,0:T(8,128)S(1)}, f32[16,16,128]{2,1,0:T(8,128)S(1)}, u32[]{:S(2)}, u32[]{:S(2)}) collective-permute-start(f32[16,16,128]{2,1,0:T(8,128)S(1)} %slice_bitcast_fusion.13.refs_4_), channel_id=1, source_target_pairs={{0,12},{1,13},{2,14},{3,15},{4,0},{5,1},{6,2},{7,3},{8,4},{9,5},{1... | collective-permute-start | bytes 393224 | tf_op jit(solution)/shard_map/ppermute | solution.py:290
  99.0 55.1 %collective-permute-start.34 = (f32[4,68,16,128]{3,2,1,0:T(8,128)}, f32[4,68,16,128]{3,2,1,0:T(8,128)}, u32[]{:S(2)}, u32[]{:S(2)}) collective-permute-start(f32[4,68,16,128]{3,2,1,0:T(8,128)} %get-tuple-element.139), channel_id=1, source_target_pairs={{0,16},{16,0},{32,48},{48,32},{64,80},{80,64},{96,112},{112,96},{1... | collective-permute-start | bytes 6684680 | tf_op jit(solution)/shard_map/ppermute | solution.py:293
  99.0 27.5 %all-to-all-start.2 = ((f32[4,52,16,128]{3,2,1,0:T(8,128)}), f32[4,52,16,128]{3,2,1,0:T(8,128)}, u32[]{:S(2)}, u32[]{:S(2)}) async-start(f32[4,52,16,128]{3,2,1,0:T(8,128)} %add.407._), calls=%async_computation.2 | async-start | bytes 3407872 | tf_op jit(solution)/shard_map/all_to_all | solution.py:304
  103.4 150.6 %all-gather.4.cloned.1.call-start = ((), (), s32[]{:S(2)}) async-start(), calls=%async_computation.5 | async-start | bytes 1966080 | tf_op jit(solution)/shard_map/all_gather | solution.py:309
  110.1 24.1 %collective-permute-start.11 = (f32[4,16,128]{2,1,0:T(8,128)S(1)}, f32[4,16,128]{2,1,0:T(8,128)S(1)}, u32[]{:S(2)}, u32[]{:S(2)}) collective-permute-start(f32[4,16,128]{2,1,0:T(8,128)S(1)} %fusion.9), channel_id=1, source_target_pairs={{0,16},{16,0},{32,48},{48,32},{64,80},{80,64},{96,112},{112,96},{1... | collective-permute-start | bytes 98312 | tf_op jit(solution)/shard_map/ppermute | solution.py:293
  128.8 146.7 %all-gather.6.cloned.1.call-start = ((), (), s32[]{:S(2)}) async-start(), calls=%async_computation.6 | async-start | bytes 2621440 | tf_op jit(solution)/shard_map/all_gather | solution.py:309
  129.9 19.9 %collective-permute-start.16 = (f32[32,16,128]{2,1,0:T(8,128)S(1)}, f32[32,16,128]{2,1,0:T(8,128)S(1)}, u32[]{:S(2)}, u32[]{:S(2)}) collective-permute-start(f32[32,16,128]{2,1,0:T(8,128)S(1)} %slice_bitcast_fusion.12.refs_5_), channel_id=1, source_target_pairs={{0,4},{1,5},{2,6},{3,7},{4,8},{5,9},{6,10},{7,11},{8,12},{9,13},{1... | collective-permute-start | bytes 786440 | tf_op jit(solution)/shard_map/ppermute | solution.py:290
  130.2 20.0 %collective-permute-start.17 = (f32[32,16,128]{2,1,0:T(8,128)S(1)}, f32[32,16,128]{2,1,0:T(8,128)S(1)}, u32[]{:S(2)}, u32[]{:S(2)}) collective-permute-start(f32[32,16,128]{2,1,0:T(8,128)S(1)} %slice_bitcast_fusion.12.refs_5_), channel_id=1, source_target_pairs={{0,8},{1,9},{2,10},{3,11},{4,12},{5,13},{6,14},{7,15},{8,0},{9,1},... | collective-permute-start | bytes 786440 | tf_op jit(solution)/shard_map/ppermute | solution.py:290
  133.5 19.4 %collective-permute-start.18 = (f32[32,16,128]{2,1,0:T(8,128)S(1)}, f32[32,16,128]{2,1,0:T(8,128)S(1)}, u32[]{:S(2)}, u32[]{:S(2)}) collective-permute-start(f32[32,16,128]{2,1,0:T(8,128)S(1)} %slice_bitcast_fusion.12.refs_5_), channel_id=1, source_target_pairs={{0,12},{1,13},{2,14},{3,15},{4,0},{5,1},{6,2},{7,3},{8,4},{9,5},{1... | collective-permute-start | bytes 786440 | tf_op jit(solution)/shard_map/ppermute | solution.py:290
  165.9 32.3 %collective-permute-start.42 = (f32[4,84,16,128]{3,2,1,0:T(8,128)}, f32[4,84,16,128]{3,2,1,0:T(8,128)}, u32[]{:S(2)}, u32[]{:S(2)}) collective-permute-start(f32[4,84,16,128]{3,2,1,0:T(8,128)} %get-tuple-element.146), channel_id=1, source_target_pairs={{0,16},{16,0},{32,48},{48,32},{64,80},{80,64},{96,112},{112,96},{1... | collective-permute-start | bytes 8257544 | tf_op jit(solution)/shard_map/ppermute | solution.py:293
  198.2 97.0 %all-gather.8.cloned.1.call-start = ((), (), s32[]{:S(2)}) async-start(), calls=%async_computation.7 | async-start | bytes 3276800 | tf_op jit(solution)/shard_map/all_gather | solution.py:309
  306.3 7.8 %collective-permute-start.51 = (f32[16,128]{1,0:T(8,128)S(1)}, f32[16,128]{1,0:T(8,128)S(1)}, u32[]{:S(2)}, u32[]{:S(2)}) collective-permute-start(f32[16,128]{1,0:T(8,128)S(1)} %get-tuple-element.220), channel_id=1, source_target_pairs={{0,12},{1,13},{2,14},{3,15},{4,0},{5,1},{6,2},{7,3},{8,4},{9,5},{1... | collective-permute-start | bytes 24584 | tf_op jit(solution)/shard_map/ppermute | solution.py:290
  307.2 9.4 %collective-permute-start.50 = (f32[16,128]{1,0:T(8,128)S(1)}, f32[16,128]{1,0:T(8,128)S(1)}, u32[]{:S(2)}, u32[]{:S(2)}) collective-permute-start(f32[16,128]{1,0:T(8,128)S(1)} %get-tuple-element.221), channel_id=1, source_target_pairs={{0,8},{1,9},{2,10},{3,11},{4,12},{5,13},{6,14},{7,15},{8,0},{9,1},... | collective-permute-start | bytes 24584 | tf_op jit(solution)/shard_map/ppermute | solution.py:290
  308.0 8.5 %collective-permute-start.49 = (f32[16,128]{1,0:T(8,128)S(1)}, f32[16,128]{1,0:T(8,128)S(1)}, u32[]{:S(2)}, u32[]{:S(2)}) collective-permute-start(f32[16,128]{1,0:T(8,128)S(1)} %get-tuple-element.222), channel_id=1, source_target_pairs={{0,4},{1,5},{2,6},{3,7},{4,8},{5,9},{6,10},{7,11},{8,12},{9,13},{1... | collective-permute-start | bytes 24584 | tf_op jit(solution)/shard_map/ppermute | solution.py:290
  309.7 19.4 %collective-permute-start.43 = (f32[5,128,128]{2,1,0:T(8,128)}, f32[5,128,128]{2,1,0:T(8,128)S(1)}, u32[]{:S(2)}, u32[]{:S(2)}) collective-permute-start(f32[5,128,128]{2,1,0:T(8,128)} %get-tuple-element.202), channel_id=1, source_target_pairs={{0,4},{1,5},{2,6},{3,7},{4,8},{5,9},{6,10},{7,11},{8,12},{9,13},{1... | collective-permute-start | bytes 983048 | tf_op jit(solution)/shard_map/ppermute | solution.py:290
  312.0 17.1 %collective-permute-start.44 = (f32[5,128,128]{2,1,0:T(8,128)}, f32[5,128,128]{2,1,0:T(8,128)S(1)}, u32[]{:S(2)}, u32[]{:S(2)}) collective-permute-start(f32[5,128,128]{2,1,0:T(8,128)} %get-tuple-element.201), channel_id=1, source_target_pairs={{0,8},{1,9},{2,10},{3,11},{4,12},{5,13},{6,14},{7,15},{8,0},{9,1},... | collective-permute-start | bytes 983048 | tf_op jit(solution)/shard_map/ppermute | solution.py:290
  314.1 15.1 %collective-permute-start.45 = (f32[5,128,128]{2,1,0:T(8,128)}, f32[5,128,128]{2,1,0:T(8,128)S(1)}, u32[]{:S(2)}, u32[]{:S(2)}) collective-permute-start(f32[5,128,128]{2,1,0:T(8,128)} %copy-done.43), channel_id=1, source_target_pairs={{0,12},{1,13},{2,14},{3,15},{4,0},{5,1},{6,2},{7,3},{8,4},{9,5},{1... | collective-permute-start | bytes 983048 | tf_op jit(solution)/shard_map/ppermute | solution.py:290
  338.4 20.7 %collective-permute-start.56 = (f32[256,512]{1,0:T(8,128)}, f32[256,512]{1,0:T(8,128)S(1)}, u32[]{:S(2)}, u32[]{:S(2)}) collective-permute-start(f32[256,512]{1,0:T(8,128)} %get-tuple-element.156._), channel_id=1, source_target_pairs={{0,1},{1,2},{2,3},{3,0},{4,5},{5,6},{6,7},{7,4},{8,9},{9,10},{10,1... | collective-permute-start | bytes 1572872 | tf_op jit(solution)/shard_map/ppermute | solution.py:288
  340.9 21.7 %collective-permute-start.58 = (f32[256,512]{1,0:T(8,128)}, f32[256,512]{1,0:T(8,128)S(1)}, u32[]{:S(2)}, u32[]{:S(2)}) collective-permute-start(f32[256,512]{1,0:T(8,128)} %get-tuple-element.163), channel_id=1, source_target_pairs={{0,3},{1,0},{2,1},{3,2},{4,7},{5,4},{6,5},{7,6},{8,11},{9,8},{10,9... | collective-permute-start | bytes 1572872 | tf_op jit(solution)/shard_map/ppermute | solution.py:288
  350.2 13.3 %collective-permute-start.72 = (f32[256,512]{1,0:T(8,128)}, f32[256,512]{1,0:T(8,128)}, u32[]{:S(2)}, u32[]{:S(2)}) collective-permute-start(f32[256,512]{1,0:T(8,128)} %get-tuple-element.173), channel_id=1, source_target_pairs={{0,4},{1,5},{2,6},{3,7},{4,8},{5,9},{6,10},{7,11},{8,12},{9,13},{1... | collective-permute-start | bytes 1572872 | tf_op jit(solution)/shard_map/ppermute | solution.py:290
  350.3 15.4 %collective-permute-start.74 = (f32[256,512]{1,0:T(8,128)}, f32[256,512]{1,0:T(8,128)S(1)}, u32[]{:S(2)}, u32[]{:S(2)}) collective-permute-start(f32[256,512]{1,0:T(8,128)} %get-tuple-element.177), channel_id=1, source_target_pairs={{0,12},{1,13},{2,14},{3,15},{4,0},{5,1},{6,2},{7,3},{8,4},{9,5},{1... | collective-permute-start | bytes 1572872 | tf_op jit(solution)/shard_map/ppermute | solution.py:290
  359.3 22.9 %collective-permute-start.57 = (f32[2,256,512]{2,1,0:T(8,128)S(1)}, f32[2,256,512]{2,1,0:T(8,128)S(1)}, u32[]{:S(2)}, u32[]{:S(2)}) collective-permute-start(f32[2,256,512]{2,1,0:T(8,128)S(1)} %pad_maximum_fusion.1), channel_id=1, source_target_pairs={{0,1},{1,2},{2,3},{3,0},{4,5},{5,6},{6,7},{7,4},{8,9},{9,10},{10,1... | collective-permute-start | bytes 3145736 | tf_op jit(solution)/shard_map/ppermute | solution.py:288
  362.8 23.3 %collective-permute-start.59 = (f32[2,256,512]{2,1,0:T(8,128)S(1)}, f32[2,256,512]{2,1,0:T(8,128)S(1)}, u32[]{:S(2)}, u32[]{:S(2)}) collective-permute-start(f32[2,256,512]{2,1,0:T(8,128)S(1)} %pad_maximum_fusion.2), channel_id=1, source_target_pairs={{0,3},{1,0},{2,1},{3,2},{4,7},{5,4},{6,5},{7,6},{8,11},{9,8},{10,9... | collective-permute-start | bytes 3145736 | tf_op jit(solution)/shard_map/ppermute | solution.py:288
  365.7 31.8 %collective-permute-start.73 = (f32[2,256,512]{2,1,0:T(8,128)}, f32[2,256,512]{2,1,0:T(8,128)}, u32[]{:S(2)}, u32[]{:S(2)}) collective-permute-start(f32[2,256,512]{2,1,0:T(8,128)} %pad_maximum_fusion.4), channel_id=1, source_target_pairs={{0,4},{1,5},{2,6},{3,7},{4,8},{5,9},{6,10},{7,11},{8,12},{9,13},{1... | collective-permute-start | bytes 3145736 | tf_op jit(solution)/shard_map/ppermute | solution.py:290
  366.8 42.0 %collective-permute-start.75 = (f32[2,256,512]{2,1,0:T(8,128)}, f32[2,256,512]{2,1,0:T(8,128)S(1)}, u32[]{:S(2)}, u32[]{:S(2)}) collective-permute-start(f32[2,256,512]{2,1,0:T(8,128)} %pad_maximum_fusion.5), channel_id=1, source_target_pairs={{0,12},{1,13},{2,14},{3,15},{4,0},{5,1},{6,2},{7,3},{8,4},{9,5},{1... | collective-permute-start | bytes 3145736 | tf_op jit(solution)/shard_map/ppermute | solution.py:290
  393.5 7.7 %collective-permute-start.61 = (f32[128,512]{1,0:T(8,128)S(1)}, f32[128,512]{1,0:T(8,128)S(1)}, u32[]{:S(2)}, u32[]{:S(2)}) collective-permute-start(f32[128,512]{1,0:T(8,128)S(1)} %add_dynamic-update-slice_fusion.3), channel_id=1, source_target_pairs={{0,4},{1,5},{2,6},{3,7},{4,8},{5,9},{6,10},{7,11},{8,12},{9,13},{1... | collective-permute-start | bytes 786440 | tf_op jit(solution)/shard_map/ppermute | solution.py:290
  405.0 9.7 %collective-permute-start.64 = (f32[128,512]{1,0:T(8,128)}, f32[128,512]{1,0:T(8,128)S(1)}, u32[]{:S(2)}, u32[]{:S(2)}) collective-permute-start(f32[128,512]{1,0:T(8,128)} %finish.2.own), channel_id=1, source_target_pairs={{0,4},{1,5},{2,6},{3,7},{4,8},{5,9},{6,10},{7,11},{8,12},{9,13},{1... | collective-permute-start | bytes 786440 | tf_op jit(solution)/shard_map/ppermute | solution.py:290
  405.1 9.7 %collective-permute-start.65 = (f32[128,512]{1,0:T(8,128)}, f32[128,512]{1,0:T(8,128)S(1)}, u32[]{:S(2)}, u32[]{:S(2)}) collective-permute-start(f32[128,512]{1,0:T(8,128)} %finish.2.own), channel_id=1, source_target_pairs={{0,12},{1,13},{2,14},{3,15},{4,0},{5,1},{6,2},{7,3},{8,4},{9,5},{1... | collective-permute-start | bytes 786440 | tf_op jit(solution)/shard_map/ppermute | solution.py:290
  420.1 7.8 %collective-permute-start.78 = (f32[64,512]{1,0:T(8,128)S(1)}, f32[64,512]{1,0:T(8,128)S(1)}, u32[]{:S(2)}, u32[]{:S(2)}) collective-permute-start(f32[64,512]{1,0:T(8,128)S(1)} %get-tuple-element.196), channel_id=1, source_target_pairs={{0,3},{1,0},{2,1},{3,2},{4,7},{5,4},{6,5},{7,6},{8,11},{9,8},{10,9... | collective-permute-start | bytes 393224 | tf_op jit(solution)/shard_map/ppermute | solution.py:288
  423.4 48.5 %collective-permute-start.68 = (f32[2,256,512]{2,1,0:T(8,128)}, f32[2,256,512]{2,1,0:T(8,128)S(1)}, u32[]{:S(2)}, u32[]{:S(2)}) collective-permute-start(f32[2,256,512]{2,1,0:T(8,128)} %get-tuple-element.190), channel_id=1, source_target_pairs={{0,1},{1,2},{2,3},{3,0},{4,5},{5,6},{6,7},{7,4},{8,9},{9,10},{10,1... | collective-permute-start | bytes 3145736 | tf_op jit(solution)/shard_map/ppermute | solution.py:288
  425.8 23.3 %collective-permute-start.77 = (f32[128,512]{1,0:T(8,128)S(1)}, f32[128,512]{1,0:T(8,128)S(1)}, u32[]{:S(2)}, u32[]{:S(2)}) collective-permute-start(f32[128,512]{1,0:T(8,128)S(1)} %add_dynamic-update-slice_fusion.1), channel_id=1, source_target_pairs={{0,1},{1,2},{2,3},{3,0},{4,5},{5,6},{6,7},{7,4},{8,9},{9,10},{10,1... | collective-permute-start | bytes 786440 | tf_op jit(solution)/shard_map/ppermute | solution.py:288
  427.8 44.1 %collective-permute-start.69 = (f32[2,256,512]{2,1,0:T(8,128)}, f32[2,256,512]{2,1,0:T(8,128)}, u32[]{:S(2)}, u32[]{:S(2)}) collective-permute-start(f32[2,256,512]{2,1,0:T(8,128)} %get-tuple-element.190), channel_id=1, source_target_pairs={{0,3},{1,0},{2,1},{3,2},{4,7},{5,4},{6,5},{7,6},{8,11},{9,8},{10,9... | collective-permute-start | bytes 3145736 | tf_op jit(solution)/shard_map/ppermute | solution.py:288
  427.9 23.4 %collective-permute-start.79 = (f32[128,512]{1,0:T(8,128)S(1)}, f32[128,512]{1,0:T(8,128)S(1)}, u32[]{:S(2)}, u32[]{:S(2)}) collective-permute-start(f32[128,512]{1,0:T(8,128)S(1)} %add_dynamic-update-slice_fusion), channel_id=1, source_target_pairs={{0,3},{1,0},{2,1},{3,2},{4,7},{5,4},{6,5},{7,6},{8,11},{9,8},{10,9... | collective-permute-start | bytes 786440 | tf_op jit(solution)/shard_map/ppermute | solution.py:288
  455.1 7.9 %collective-permute-start.81 = (f32[128,512]{1,0:T(8,128)}, f32[128,512]{1,0:T(8,128)S(1)}, u32[]{:S(2)}, u32[]{:S(2)}) collective-permute-start(f32[128,512]{1,0:T(8,128)} %finish.3.own), channel_id=1, source_target_pairs={{0,3},{1,0},{2,1},{3,2},{4,7},{5,4},{6,5},{7,6},{8,11},{9,8},{10,9... | collective-permute-start | bytes 786440 | tf_op jit(solution)/shard_map/ppermute | solution.py:288
  463.0 7.7 %collective-permute-start.83 = (f32[64,512]{1,0:T(8,128)S(1)}, f32[64,512]{1,0:T(8,128)S(1)}, u32[]{:S(2)}, u32[]{:S(2)}) collective-permute-start(f32[64,512]{1,0:T(8,128)S(1)} %slice.443), channel_id=1, source_target_pairs={{0,3},{1,0},{2,1},{3,2},{4,7},{5,4},{6,5},{7,6},{8,11},{9,8},{10,9... | collective-permute-start | bytes 393224 | tf_op jit(solution)/shard_map/ppermute | solution.py:288
  471.9 9.2 %collective-permute-start.70 = (f32[256,512]{1,0:T(8,128)S(1)}, f32[256,512]{1,0:T(8,128)S(1)}, u32[]{:S(2)}, u32[]{:S(2)}) collective-permute-start(f32[256,512]{1,0:T(8,128)S(1)} %slice_bitcast_fusion.7), channel_id=1, source_target_pairs={{0,1},{1,2},{2,3},{3,0},{4,5},{5,6},{6,7},{7,4},{8,9},{9,10},{10,1... | collective-permute-start | bytes 1572872 | tf_op jit(solution)/shard_map/ppermute | solution.py:288
  473.1 10.7 %collective-permute-start.71 = (f32[256,512]{1,0:T(8,128)S(1)}, f32[256,512]{1,0:T(8,128)S(1)}, u32[]{:S(2)}, u32[]{:S(2)}) collective-permute-start(f32[256,512]{1,0:T(8,128)S(1)} %slice_bitcast_fusion.6), channel_id=1, source_target_pairs={{0,3},{1,0},{2,1},{3,2},{4,7},{5,4},{6,5},{7,6},{8,11},{9,8},{10,9... | collective-permute-start | bytes 1572872 | tf_op jit(solution)/shard_map/ppermute | solution.py:288
  486.2 21.8 %collective-permute-start.84 = (f32[2,256,512]{2,1,0:T(8,128)}, f32[2,256,512]{2,1,0:T(8,128)S(1)}, u32[]{:S(2)}, u32[]{:S(2)}) collective-permute-start(f32[2,256,512]{2,1,0:T(8,128)} %get-tuple-element.184), channel_id=1, source_target_pairs={{0,4},{1,5},{2,6},{3,7},{4,8},{5,9},{6,10},{7,11},{8,12},{9,13},{1... | collective-permute-start | bytes 3145736 | tf_op jit(solution)/shard_map/ppermute | solution.py:290
  486.2 21.9 %collective-permute-start.85 = (f32[2,256,512]{2,1,0:T(8,128)}, f32[2,256,512]{2,1,0:T(8,128)}, u32[]{:S(2)}, u32[]{:S(2)}) collective-permute-start(f32[2,256,512]{2,1,0:T(8,128)} %get-tuple-element.184), channel_id=1, source_target_pairs={{0,12},{1,13},{2,14},{3,15},{4,0},{5,1},{6,2},{7,3},{8,4},{9,5},{1... | collective-permute-start | bytes 3145736 | tf_op jit(solution)/shard_map/ppermute | solution.py:290
  508.1 10.5 %collective-permute-start.86 = (f32[256,512]{1,0:T(8,128)S(1)}, f32[256,512]{1,0:T(8,128)S(1)}, u32[]{:S(2)}, u32[]{:S(2)}) collective-permute-start(f32[256,512]{1,0:T(8,128)S(1)} %slice_bitcast_fusion.1), channel_id=1, source_target_pairs={{0,4},{1,5},{2,6},{3,7},{4,8},{5,9},{6,10},{7,11},{8,12},{9,13},{1... | collective-permute-start | bytes 1572872 | tf_op jit(solution)/shard_map/ppermute | solution.py:290
  509.2 10.1 %collective-permute-start.87 = (f32[256,512]{1,0:T(8,128)S(1)}, f32[256,512]{1,0:T(8,128)S(1)}, u32[]{:S(2)}, u32[]{:S(2)}) collective-permute-start(f32[256,512]{1,0:T(8,128)S(1)} %slice_bitcast_fusion), channel_id=1, source_target_pairs={{0,12},{1,13},{2,14},{3,15},{4,0},{5,1},{6,2},{7,3},{8,4},{9,5},{1... | collective-permute-start | bytes 1572872 | tf_op jit(solution)/shard_map/ppermute | solution.py:290
  (94 other events, 571.5 us)
Sparse Core Ops, SparseCore 0:
  129.0 29.5 all-gather.3
  198.3 28.1 all-gather.5
  238.1 32.4 all-gather.7

commit v3 on v2

v3 whole, which is shorter than its diff:
```python
import functools

import jax
import jax.numpy as jnp
from jax import lax
from jax.experimental import pallas as pl
from jax.experimental.pallas import tpu as pltpu
from jax.sharding import PartitionSpec as P

F32 = jnp.float32
BF16 = jnp.bfloat16
STEPS = 6
V, H, S = (pl.BlockSpec(memory_space=m) for m in (pltpu.VMEM, pltpu.HBM, pltpu.SMEM))


def split(value):
    high = value.astype(BF16)
    return high, (value - high.astype(F32)).astype(BF16)


def dot(a, b):
    return jnp.dot(a, b, preferred_element_type=F32)


def call(kernel, name, mib, inputs, outputs, scratch=()):
    specs, operands = zip(*inputs)
    return pl.pallas_call(
        kernel,
        in_specs=specs,
        out_specs=[V] * len(outputs),
        out_shape=[jax.ShapeDtypeStruct(*o) for o in outputs],
        scratch_shapes=scratch,
        compiler_params=pltpu.CompilerParams(vmem_limit_bytes=mib << 20),
        name=name,
    )(*operands)


def fetch(pairs, sems):
    copies = [pltpu.make_async_copy(a, b, sems.at[i]) for i, (a, b) in enumerate(pairs)]
    for copy in copies:
        copy.start()
    return copies


def gram_kernel(rows, extra, whole, meta, scale, inverse, rhs, tiles, *refs):
    outs = refs[-6:-5] if whole else refs[-7:-5]
    d_buf, r_buf, t_buf, product, sems = refs[-5:]
    x, y, u, z = meta[0], meta[1], meta[2], meta[3]
    blocks = extra + rows
    group = pl.ds(pl.multiple_of(z * 128, 128), 128)
    copies = []
    sem = 0
    for i, b in enumerate(blocks):
        copies.append(fetch([(inverse.at[b], d_buf.at[i]), (rhs.at[b, :, group], r_buf.at[i])], sems.at[pl.ds(sem, 2)]))
        sem += 2
    base = 0
    for s in rows:
        copies[len(extra) + rows.index(s)] += fetch(
            [(tiles.at[s, pl.ds(0, s)], t_buf.at[pl.ds(base, s)])], sems.at[pl.ds(sem, 1)]
        )
        sem += 1
        base += s

    def store(slot, row, at):
        for yy in range(4):
            if whole:
                for core in range(2):
                    outs[0][2 * yy + core, at] = product[slot, pl.ds(pl.multiple_of(row + yy * 32 + core * 16, 16), 16), :]
            else:
                ey = lax.rem(yy + 4 - y, 4) if extra else yy
                start = row + yy * 32
                outs[0][ey, at] = product[slot, pl.ds(pl.multiple_of(start + u * 16, 16), 16), :]
                outs[1][ey, at] = product[slot, pl.ds(pl.multiple_of(start + (1 - u) * 16, 16), 16), :]

    turn = 0
    base = 0
    unit = 4 * len(blocks)
    for i, b in enumerate(blocks):
        for copy in copies[i]:
            copy.wait()
        high, low = split(r_buf[i])
        both = jnp.concatenate([high, low], axis=0)
        slot = turn % 2
        turn += 1
        for dz in range(4):
            chunk = lax.rem(z + 4 - dz, 4) * 4 + x
            part = d_buf[i, pl.ds(pl.multiple_of(chunk * 128, 128), 128), :]
            product[slot, pl.ds(dz * 128, 128), :] = dot(jnp.concatenate([part, part], axis=1), both)
            store(slot, dz * 128, i * 4 + dz)
        if b not in rows:
            continue
        for j in range(b):
            slot = turn % 2
            turn += 1
            product[slot] = dot(d_buf[i], t_buf[base]) * scale[b, j]
            base += 1
            for zz in range(4):
                for ex in range(4):
                    store(slot, (zz * 4 + lax.rem(x + ex, 4)) * 128, unit + ex * 4 + zz)
            unit += 16


def gram(rows, extra, whole, meta, scale, inverse, rhs, tiles, *after):
    n = len(extra) + len(rows)
    units = 4 * n + 16 * sum(rows)
    outputs = [((8, units, 16, 128), F32)] if whole else [((4, units, 16, 128), F32)] * 2
    return call(
        functools.partial(gram_kernel, rows, extra, whole),
        "gram",
        58,
        [(S, meta), (S, scale), (H, inverse), (H, rhs), (H, tiles)] + [(H, a) for a in after],
        outputs,
        [
            pltpu.VMEM((n, 2048, 256), BF16),
            pltpu.VMEM((n, 256, 128), F32),
            pltpu.VMEM((sum(rows), 256, 128), BF16),
            pltpu.VMEM((2, 2048, 128), F32),
            pltpu.SemaphoreType.DMA((2 * n + len(rows),)),
        ],
    )


def step_kernel(count, meta, *refs):
    y, u, z = meta[1], meta[2], meta[3]
    pieces, refs = refs[:4], refs[4:]
    older, refs = refs[: count - 1], refs[count - 1 :]
    gram_refs, refs = refs[:-7], refs[-7:]
    chunks, solved, g_buf, sems = refs[:4], refs[4], refs[5], refs[6]
    targets = [g_buf.at[d] for d in (0, 1, 3, 2)]
    if len(gram_refs) == 5:
        targets[3:] = [g_buf.at[2, pl.ds(0, 8 * count)], g_buf.at[2, pl.ds(8 * count, 8 * count)]]
    copies = fetch(list(zip(gram_refs, targets)), sems)
    for ey in range(4):
        row = lax.rem(y + 4 - ey, 4) * 32
        for eu in range(2):
            at = pl.multiple_of(row + (u + eu - 2 * u * eu) * 16, 16)
            for dz in range(4):
                solved[dz, pl.ds(at, 16), :] = pieces[ey][eu, dz]
    for copy in copies:
        copy.wait()
    total = jnp.zeros((256, 128), F32)
    for j in range(count):
        block = jnp.concatenate([g_buf[d, pl.ds(16 * j, 16)].reshape(256, 128) for d in range(4)], axis=1)
        source = solved if j == count - 1 else older[j]
        a_high, a_low = split(block)
        b_high, b_low = split(source[...].reshape(512, 128))
        total = total + (dot(a_high, b_high) + (dot(a_high, b_low) + dot(a_low, b_high)))
    total = total.reshape(4, 4, 16, 128)
    for ex in range(4):
        for zz in range(4):
            chunks[ex][lax.rem(z + 4 - zz, 4)] = total[ex, zz]


def step(meta, pieces, older, pieces_z):
    count = len(older) + 1
    *chunks, solved = call(
        functools.partial(step_kernel, count),
        "step",
        24,
        [(S, meta)] + [(V, p) for p in pieces] + [(V, o) for o in older] + [(H, g) for g in pieces_z],
        [((4, 16, 128), F32)] * 4 + [((4, 128, 128), F32)],
        [pltpu.VMEM((4, 16 * count, 16, 128), F32), pltpu.SemaphoreType.DMA((5,))],
    )
    return chunks, solved


def early_kernel(meta, *refs):
    z = meta[3]
    own, others, solved, both = refs[:5], refs[5:8], refs[8], refs[9]
    for k in range(5):
        for d in range(4):
            at = pl.multiple_of(lax.rem(z + 4 - d, 4) * 128, 128)
            value = own[k][0] if d == 0 else others[d - 1][k]
            high, low = split(value)
            solved[k, :, pl.ds(at, 128)] = value
            both[k, pl.ds(0, 128), pl.ds(at, 128)] = high
            both[k, pl.ds(128, 128), pl.ds(at, 128)] = low


def early(meta, own, others):
    return call(
        early_kernel,
        "early",
        16,
        [(S, meta)] + [(V, o) for o in own] + [(V, o) for o in others],
        [((5, 128, 512), F32), ((5, 256, 512), BF16)],
    )


def late_kernel(meta, a, b, c, d, solved, both):
    y, u, z = meta[1], meta[2], meta[3]
    for ey, piece in enumerate((a, b, c, d)):
        row = lax.rem(y + 4 - ey, 4) * 32
        for eu in range(2):
            at = pl.multiple_of(row + (u + eu - 2 * u * eu) * 16, 16)
            low_at = pl.multiple_of(at + 128, 16)
            for dz in range(4):
                group = pl.ds(pl.multiple_of(lax.rem(z + 4 - dz, 4) * 128, 128), 128)
                value = piece[eu, dz]
                high, low = split(value)
                solved[0, pl.ds(at, 16), group] = value
                both[0, pl.ds(at, 16), group] = high
                both[0, pl.ds(low_at, 16), group] = low


def late(meta, pieces):
    return call(
        late_kernel,
        "late",
        8,
        [(S, meta)] + [(V, p) for p in pieces],
        [((1, 128, 512), F32), ((1, 256, 512), BF16)],
    )


def trail_kernel(first, scale, tiles, early_both, late_both, *refs):
    outs, t_buf, sems = refs[:-2], refs[-2], refs[-1]
    count = sum(out.shape[0] for out in outs)
    copies = fetch([(tiles.at[first[i]], t_buf.at[i]) for i in range(count)], sems)
    i = 0
    for out in outs:
        for block in range(out.shape[0]):
            copies[i].wait()
            total = None
            for k in range(STEPS):
                own = t_buf[i, k]
                value = early_both[k] if k < 5 else late_both[0]
                part = dot(jnp.concatenate([own, own], axis=1), value) * scale[first[i], k]
                total = part if total is None else total + part
            out[block] = total
            i += 1


def trail_first_kernel(first, scale, tiles, early_both, late_both, *refs):
    trail_kernel(first, scale, tiles, early_both, late_both, *refs)


def trail_rest_kernel(first, scale, tiles, early_both, late_both, _, *refs):
    trail_kernel(first, scale, tiles, early_both, late_both, *refs)


def trail(first, scale, tiles, early_both, late_both, blocks, *after):
    count = first.shape[0]
    return call(
        trail_rest_kernel if after else trail_first_kernel,
        "trail",
        24 if after else 58,
        [(S, first), (S, scale), (H, tiles), (V, early_both), (V, late_both)] + [(H, a) for a in after],
        [((blocks, 256, 512), F32)] * (count // blocks),
        [pltpu.VMEM((count, 6, 256, 128), BF16), pltpu.SemaphoreType.DMA((count,))],
    )


def sum_sub_kernel(where, *refs):
    for h in range(2):
        a, b, c = refs[3 * h : 3 * h + 3]
        outs = refs[6 + 5 * h : 11 + 5 * h]

        def rows(e):
            at = lax.rem(where[h] + e, 4)
            return a[at] + (b[at] + c[at])

        outs[0][...] = rows(0)
        outs[1][...] = rows(1)
        outs[2][...] = rows(3)
        far = rows(2)
        outs[3][...] = far[:64]
        outs[4][...] = far[64:]


def sum_sub(where, parts):
    outputs = [((128, 512), F32)] * 3 + [((64, 512), F32)] * 2
    return call(sum_sub_kernel, "sum_sub", 32, [(S, where)] + [(V, p) for p in parts], outputs * 2)


def finish_kernel(at, rhs, *refs):
    parts, outs, buf, sems = refs[:6], refs[6:8], refs[8], refs[9]
    copies = fetch(
        [(rhs.at[at[2 * h], pl.ds(pl.multiple_of(at[2 * h + 1] * 128, 128), 128)], buf.at[h]) for h in range(2)], sems
    )
    for h in range(2):
        a, b, c = parts[3 * h : 3 * h + 3]
        copies[h].wait()
        outs[h][...] = buf[h] - (a[...] + (b[...] + c[...]))


def finish(at, rhs, parts):
    return call(
        finish_kernel,
        "finish",
        54,
        [(S, at), (H, rhs)] + [(V, p) for p in parts],
        [((128, 512), F32)] * 2,
        [pltpu.VMEM((2, 128, 512), F32), pltpu.SemaphoreType.DMA((2,))],
    )


def place_kernel(where, *refs):
    for h in range(2):
        own, back, ahead, low, high = refs[5 * h : 5 * h + 5]
        out = refs[10 + h]
        for e, ref in ((0, own), (3, back), (1, ahead)):
            out[lax.rem(where[h] + e, 4)] = ref[...]
        far = lax.rem(where[h] + 2, 4)
        out[far, pl.ds(0, 64), :] = low[...]
        out[far, pl.ds(64, 64), :] = high[...]


def place(where, parts):
    return call(place_kernel, "place", 16, [(S, where)] + [(V, p) for p in parts], [((4, 128, 512), F32)] * 2)


def write_kernel(starts, *refs):
    count = (len(refs) - 2) if len(refs) % 2 == 0 else (len(refs) - 3)
    values, out, sems = refs[:count], refs[-2], refs[-1]
    copies = fetch([(value, out.at[pl.ds(starts[i], value.shape[0])]) for i, value in enumerate(values)], sems)
    for copy in copies:
        copy.wait()


def write(starts, values, out=None):
    operands = [starts] + list(values) + ([] if out is None else [out])
    return pl.pallas_call(
        write_kernel,
        in_specs=[S] + [H] * (len(operands) - 1),
        out_specs=H,
        out_shape=jax.ShapeDtypeStruct((16, 256, 512), F32),
        scratch_shapes=[pltpu.SemaphoreType.DMA((len(values),))],
        input_output_aliases={} if out is None else {len(operands) - 1: 0},
        name="write",
    )(*operands)


def on_device(rhs_blocks, factor_tiles, tile_scale, diag_inverse):
    row, column = lax.axis_index("prow"), lax.axis_index("pcol")
    y, u, z, x = row // 2, row % 2, column // 4, column % 4
    meta = jnp.stack([x, y, u, z]).astype(jnp.int32)
    tiles = jnp.transpose(factor_tiles, (0, 2, 1, 3))

    def shift(value, axis, d):
        if axis == "x":
            return lax.ppermute(value, "pcol", [(i, i // 4 * 4 + (i + d) % 4) for i in range(16)])
        if axis == "z":
            return lax.ppermute(value, "pcol", [(i, (i + 4 * d) % 16) for i in range(16)])
        if axis == "y":
            return lax.ppermute(value, "prow", [(i, (i + 2 * d) % 8) for i in range(8)])
        return lax.ppermute(value, "prow", [(i, i ^ 1) for i in range(8)])

    def exchange(values, axis):
        return [values[0]] + [shift(values[d], axis, d) for d in (1, 2, 3)]

    def spread(value, axis):
        return exchange([value] * 4, axis)

    def ring(values):
        return [(shift(up, axis, 1), shift(down, axis, 3)) for axis, up, down in values]

    def ring_z(value):
        half = value.shape[0] // 2
        near = ring([("z", value, value)])[0]
        far = ring([("z", near[0][:half], near[1][half:])])[0]
        return (value,) + near + far

    def make(rows, extra, whole, *after):
        return gram(rows, extra, whole, meta, tile_scale, diag_inverse, rhs_blocks, tiles, *after)

    def gather(piece):
        both = jnp.stack([piece, shift(piece, "core", 1)])
        return both, spread(both, "y")

    keep, send = make((1,), (0,), False)
    half = keep + shift(send, "core", 1)
    a, b, c, d = exchange([half[i] for i in range(4)], "y")
    total = (a + b) + (c + d)
    start = {0: total[:4], 1: total[4:8]}
    a, b, c, d = spread(total[8:], "z")
    grams = {1: (a, b, d, c)}

    keep, send = make((2,), (), False, keep)
    half_2 = keep + shift(send, "core", 1)
    groups = [[2 * i + core for i in range(4)] for core in range(2)]
    parts = lax.all_to_all(half_2, "prow", 0, 0, axis_index_groups=groups)
    total = (parts[0] + parts[1]) + (parts[2] + parts[3])
    start[2] = total[:4]
    grams[2] = ring_z(total[4:])

    total = lax.psum_scatter(make((3, 4), (), True, half, keep)[0], "prow")
    start[3], start[4] = total[:4], total[4:8]
    grams[3], grams[4] = ring_z(total[8:56]), ring_z(total[56:])

    solved = []
    piece = start[0]
    for s in range(1, STEPS):
        both, pieces = gather(piece)
        if s == 1:
            total = lax.psum_scatter(make((5,), (), True, both)[0], "prow")
            start[5] = total[:4]
            grams[5] = ring_z(total[4:])
        chunks, latest = step(meta, pieces, solved, grams[s])
        solved.append(latest)
        a, b, c, d = exchange(chunks, "x")
        piece = start[s] - ((a + b) + (c + d))

    others = exchange([jnp.stack([v[-d % 4] for v in solved]) for d in range(4)], "z")[1:]
    solved_early, both_early = early(meta, solved, others)
    piece = jnp.stack(exchange([piece[-d % 4] for d in range(4)], "z"))
    solved_late, both_late = late(meta, gather(piece)[1])

    axes = (("x", "z", x, z, 6), ("z", "x", z, x, 14))
    one, two = [a[0] for a in axes], [a[1] for a in axes]
    where = jnp.stack([a[3] for a in axes]).astype(jnp.int32)

    def chunks_of(offsets, blocks, *after):
        first = jnp.stack([base + 2 * ((me + d) % 4) + i for d in offsets for _, _, me, _, base in axes for i in range(2)])
        return trail(first.astype(jnp.int32), tile_scale, tiles, both_early, both_late, blocks, *after)

    far = chunks_of((2,), 1)
    near = chunks_of((1, 3, 0), 2, far[0])
    moved = ring([(one[h], far[2 * h], far[2 * h + 1]) for h in range(2)])
    ups = [near[h].at[:1].add(moved[h][0]) for h in range(2)]
    downs = [near[2 + h].at[1:].add(moved[h][1]) for h in range(2)]
    moved = ring([(one[h], ups[h], downs[h]) for h in range(2)])
    terms = [v.reshape(4, 128, 512) for h in range(2) for v in (near[4 + h],) + moved[h]]
    subs = sum_sub(where, terms)
    subs = [subs[:5], subs[5:]]
    moved = ring([(two[h], subs[h][3], subs[h][4]) for h in range(2)])
    ups = [subs[h][1].at[:64].add(moved[h][0]) for h in range(2)]
    downs = [subs[h][2].at[64:].add(moved[h][1]) for h in range(2)]
    moved = ring([(two[h], ups[h], downs[h]) for h in range(2)])
    at = jnp.stack([v for _, _, me, other, base in axes for v in (base + 2 * me + other // 2, other % 2)])
    done = finish(at.astype(jnp.int32), rhs_blocks, [v for h in range(2) for v in (subs[h][0],) + moved[h]])
    near = ring([(two[h], done[h], done[h]) for h in range(2)])
    far = ring([(two[h], near[h][0][:64], near[h][1][64:]) for h in range(2)])
    own = place(where, [v for h in range(2) for v in (done[h],) + near[h] + far[h]])
    own = [v.reshape(2, 256, 512) for v in own]
    near = ring([(one[h], own[h], own[h]) for h in range(2)])
    far = ring([(one[h], near[h][0][:1], near[h][1][1:]) for h in range(2)])
    at = jnp.stack([base - 6 + 2 * ((me + d) % 4) for _, _, me, _, base in axes for d in (0, 3, 1)])
    trailing = write(at.astype(jnp.int32), [v for h in range(2) for v in (own[h],) + near[h]])
    at = jnp.stack([base - 6 + 2 * ((me + 2) % 4) + i for _, _, me, _, base in axes for i in range(2)])
    trailing = write(at.astype(jnp.int32), [v for h in range(2) for v in far[h]], trailing)
    return jnp.concatenate([solved_early, solved_late]), trailing


def solution(mesh):
    in_specs = (P(None, "prow", None), P(None, "prow", None, "pcol"), P(), P(None, None, "prow"))
    out_specs = (P(None, "pcol", None), P(None, "prow", None))
    return jax.shard_map(
        on_device, mesh=mesh, in_specs=in_specs, out_specs=out_specs, check_vma=False
    )
```

time: 537 us -> 658 us (1.23)
  Pallas kernels: 60.3 us -> 315 us
  blocking collectives: 66.8 us -> 0 us
  local copies, waits for them, and re-layouts: 57.2 us -> 29.1 us
  waiting for transfers between devices: 168 us -> 144 us
  other arithmetic: 28.3 us -> 10.8 us
    pallas_call x0 -> x2, Pallas kernels: none -> 258 us  [write(): pl.pallas_call(write_kernel, in_specs=[S] + [H] * (len(operands) - 1), ou...]
    all_to_all x2 -> x0, blocking collectives: 66.8 us -> none  [reduce_rows(): parts = lax.all_to_all(half, 'prow', 0, 0, axis_index_groups=groups)]
    ppermute x31, waiting for transfers between devices: 66 us -> 21.8 us  [shift(): lax.ppermute(value, 'pcol', [(i, i // 4 * 4 + (i + d) % 4) for i in range...]
    ppermute x28 -> x41, waiting for transfers between devices: 34.8 us -> 58.2 us  [shift(): lax.ppermute(value, 'pcol', [(i, (i + 4 * d) % 16) for i in range(16)])]
    ppermute x18 -> x21, waiting for transfers between devices: 41 us -> 59.1 us  [shift(): return lax.ppermute(value, 'prow', [(i, (i + 2 * d) % 8) for i in range(8)])]
    unnamed x101 -> x73, local copies, waits for them, and re-layouts: 37.8 us -> 19.8 us
    all_to_all x3 -> x1, waiting for transfers between devices: 17.4 us -> 0.01 us  [on_device(): parts = lax.all_to_all(half_2, 'prow', 0, 0, axis_index_groups=groups)]
    add x10 -> x4, other arithmetic: 17.2 us -> 2.29 us  [the longest x1 1.17 us: on_device(): half_2 = keep + shift(send, 'core', 1)]
  transfers between devices with their start and end apart: 94 -> 104, of which waited for: 54 -> 52; matrix products, arithmetic and copies ran while one was open for 8% -> 3% of each run, Pallas kernels for 8% -> 34%
where the time goes in v3:
time: 658 us; the launch traced here: 647 us
  Pallas kernels  315 us (48%)
  waiting for transfers between devices  144 us (22%)
  starting transfers between devices  132 us (20%)
  local copies, waits for them, and re-layouts  29.1 us (4%)
  between operations  15.3 us (2%)
  other arithmetic  10.8 us (2%)
    pallas_call x2, Pallas kernels, write(): pl.pallas_call(write_kernel, in_specs=[S] + [H] * (len(operands) - 1), ou...  258 us
    ppermute x41, starting transfers between devices, shift(): lax.ppermute(value, 'pcol', [(i, (i + 4 * d) % 16) for i in range(16)])  60.5 us
    ppermute x21, waiting for transfers between devices, shift(): return lax.ppermute(value, 'prow', [(i, (i + 2 * d) % 8) for i in range(8)])  59.1 us
    ppermute x41, waiting for transfers between devices, shift(): lax.ppermute(value, 'pcol', [(i, (i + 4 * d) % 16) for i in range(16)])  58.2 us
    pallas_call x16, Pallas kernels, call(): pl.pallas_call(kernel, in_specs=specs, out_specs=[V] * len(outputs), out_...  57.5 us
    ppermute x31, starting transfers between devices, shift(): lax.ppermute(value, 'pcol', [(i, i // 4 * 4 + (i + d) % 4) for i in range...  43.1 us
    ppermute x21, starting transfers between devices, shift(): return lax.ppermute(value, 'prow', [(i, (i + 2 * d) % 8) for i in range(8)])  24 us
    ppermute x31, waiting for transfers between devices, shift(): lax.ppermute(value, 'pcol', [(i, i // 4 * 4 + (i + d) % 4) for i in range...  21.8 us
  transfers between devices with their start and end apart: 104, of which 52 were waited for; matrix products, arithmetic and copies ran while one was open for 3% of the time, Pallas kernels for 34%

profile of v3, /device:TPU:6, one launch (start us, length us, event | category | flops | bytes accessed | tf_op | source)
XLA Modules:
  0.0 647.2 jit_solution(10862040054521687071)
XLA Ops:
  9.2 4.2 gram.4
  13.6 4.8 gram.5
  19.4 9.3 %gram.6 = f32[8,120,16,128]{3,2,1,0:T(8,128)} custom-call(s32[4]{0:T(128)} %pad_add_fusion.meta, f32[22,6]{1,0:T(8,128)} %copy.7.scale, bf16[6,2048,256]{2,1,0:T(8,128)(2,1)} %inverse.7, f32[22,256,512]{2,1,0:T(8,128)} %rhs.17, bf16[22,6,256,128]{3,2,1,0:T(8,128)(2,1)} %bitcast.104, f32[4,24,16,128]{3,2,1,0:T(8,128)} %add.330.refs_0_, ...), custom_call_target="tpu_custom_call" | custom-call | tf_op jit(solution)/shard_map/gram/pallas_call | solution.py:27
  29.9 3.1 collective-permute-start.3
  34.6 8.3 %collective-permute-done.3 = f32[24,16,128]{2,1,0:T(8,128)S(1)} collective-permute-done((f32[24,16,128]{2,1,0:T(8,128)S(1)}, f32[24,16,128]{2,1,0:T(8,128)S(1)}, u32[]{:S(2)}, u32[]{:S(2)}) %collective-permute-start.3) | collective-permute-done | bytes 196640 | tf_op jit(solution)/shard_map/ppermute | solution.py:346
  42.9 4.1 collective-permute-done.1
  49.0 6.8 %gram.7 = f32[8,84,16,128]{3,2,1,0:T(8,128)} custom-call(s32[4]{0:T(128)} %pad_add_fusion.meta, f32[22,6]{1,0:T(8,128)} %copy.7.scale, bf16[6,2048,256]{2,1,0:T(8,128)(2,1)} %inverse.7, f32[22,256,512]{2,1,0:T(8,128)} %rhs.17, bf16[22,6,256,128]{3,2,1,0:T(8,128)(2,1)} %bitcast.105, f32[2,4,16,128]{3,2,1,0:T(8,128)} %pad_maximum_fusion.1.refs_0_), custom_call_target="tpu_custom_call" | custom-call | tf_op jit(solution)/shard_map/gram/pallas_call | solution.py:27
  57.3 2.7 collective-permute-done.18
  61.2 3.7 all-to-all-start
  64.9 3.2 collective-permute-start.7
  68.1 4.5 collective-permute-start.10
  75.4 14.2 %collective-permute-done.7.refs_3_ = f32[2,4,16,128]{3,2,1,0:T(8,128)S(1)} collective-permute-done((f32[2,4,16,128]{3,2,1,0:T(8,128)S(1)}, f32[2,4,16,128]{3,2,1,0:T(8,128)S(1)}, u32[]{:S(2)}, u32[]{:S(2)}) %collective-permute-start.7) | collective-permute-done | bytes 65568 | tf_op jit(solution)/shard_map/ppermute | solution.py:346
  90.8 5.3 collective-permute-done.5.refs_1_
  100.8 4.7 collective-permute-start.20
  105.9 3.4 collective-permute-done.20.refs_7_
  109.3 3.8 collective-permute-start.22
  122.9 3.3 collective-permute-start.23
  128.7 3.3 collective-permute-start.31
  133.2 3.3 collective-permute-start.42
  138.4 3.3 collective-permute-start.33
  143.3 4.4 collective-permute-done.28.refs_2_
  148.3 4.9 collective-permute-done.27.refs_1_
  153.2 3.2 collective-permute-done.32.refs_9_
  163.2 3.2 collective-permute-done.35
  192.5 2.8 collective-permute-start.55
  201.1 3.8 collective-permute-done.54.refs_11_
  216.2 2.8 collective-permute-start.64
  228.8 3.1 collective-permute-done.68.d
  234.6 3.2 collective-permute-done.66.b
  243.0 5.6 trail.2
  254.6 3.5 copy-done
  259.1 10.1 %trail.3 = (f32[2,256,512]{2,1,0:T(8,128)S(1)}, f32[2,256,512]{2,1,0:T(8,128)S(1)}, f32[2,256,512]{2,1,0:T(8,128)S(1)}, f32[2,256,512]{2,1,0:T(8,128)S(1)}, f32[...) custom-call(s32[12]{0:T(128)S(1)} %stack.253.first, f32[22,6]{1,0:T(8,128)S(1)} %copy-done.7, ...), custom_call_target="tpu_custom_call" | custom-call | tf_op jit(solution)/shard_map/trail/pallas_call | solution.py:27
  270.4 3.5 collective-permute-start.76
  274.5 3.3 collective-permute-start.70
  277.9 15.0 %collective-permute-done.76 = f32[2,256,512]{2,1,0:T(8,128)S(1)} collective-permute-done((f32[2,256,512]{2,1,0:T(8,128)S(1)}, f32[2,256,512]{2,1,0:T(8,128)S(1)}, u32[]{:S(2)}, u32[]{:S(2)}) %collective-permute-start.76) | collective-permute-done | bytes 1048608 | tf_op jit(solution)/shard_map/ppermute | solution.py:344
  292.9 3.6 collective-permute-done.74
  299.1 3.2 collective-permute-start.79
  302.3 3.2 collective-permute-start.81
  309.4 3.8 collective-permute-start.82
  319.7 4.1 collective-permute-done.78.refs_1_
  324.5 3.2 finish.1
  329.9 3.2 collective-permute-start.89
  337.8 3.3 collective-permute-start.91
  350.1 3.3 collective-permute-start.93
  353.4 15.1 %collective-permute-done.99.refs_5_ = f32[2,256,512]{2,1,0:T(8,128)S(1)} collective-permute-done((f32[2,256,512]{2,1,0:T(8,128)S(1)}, f32[2,256,512]{2,1,0:T(8,128)S(1)}, u32[]{:S(2)}, u32[]{:S(2)}) %collective-permute-start.99) | collective-permute-done | bytes 1048608 | tf_op jit(solution)/shard_map/ppermute | solution.py:344
  375.3 3.4 collective-permute-start.94
  381.1 192.4 %write.2.refs_4_ = f32[16,256,512]{2,1,0:T(8,128)} custom-call(s32[6]{0:T(128)} %stack.265.starts, f32[2,256,512]{2,1,0:T(8,128)} %bitcast.110, f32[2,256,512]{2,1,0:T(8,128)} %copy-done.25, f32[2,256,512]{2,1,0:T(8,128)} %copy-done.24, f32[2,256,512]{2,1,0:T(8,128)} %bitcast.113, f32[2,256,512]{2,1,0:T(8,128)} %copy-done.23, f32[2,256,512]{2,1,0:T(8,128)} %copy-done.22), custom_call_target="tpu_custom_call" | custom-call | tf_op jit(solution)/shard_map/write/pallas_call | solution.py:323
  574.7 65.3 %write.3 = f32[16,256,512]{2,1,0:T(8,128)} custom-call(s32[4]{0:T(128)} %pad_add_fusion.1.starts, f32[1,256,512]{2,1,0:T(8,128)} %collective-permute-done.94.refs_0_, f32[1,256,512]{2,1,0:T(8,128)} %copy-done.28, f32[1,256,512]{2,1,0:T(8,128)} %copy-done.27, f32[1,256,512]{2,1,0:T(8,128)} %copy-done.26, ...), custom_call_target="tpu_custom_call", output_to_operand_aliasing={{}: (5, {})} | custom-call | tf_op jit(solution)/shard_map/write/pallas_call | solution.py:323
  (310 shorter events, 153.1 us)
Async XLA Ops:
  7.2 120.5 %reduce-scatter.3.cloned.1.call-start = ((), (), s32[]{:S(2)}) async-start(), calls=%async_computation.3 | async-start | bytes 8847360 | tf_op jit(solution)/shard_map/reduce_scatter | solution.py:387
  28.8 146.4 %reduce-scatter.5.cloned.1.call-start = ((), (), s32[]{:S(2)}) async-start(), calls=%async_computation.4 | async-start | bytes 6193152 | tf_op jit(solution)/shard_map/reduce_scatter | solution.py:396
  29.9 13.0 %collective-permute-start.3 = (f32[24,16,128]{2,1,0:T(8,128)S(1)}, f32[24,16,128]{2,1,0:T(8,128)S(1)}, u32[]{:S(2)}, u32[]{:S(2)}) collective-permute-start(f32[24,16,128]{2,1,0:T(8,128)S(1)} %get-tuple-element.212), channel_id=1, source_target_pairs={{0,96},{16,112},{32,0},{48,16},{64,32},{80,48},{96,64},{112,80},{1... | collective-permute-start | bytes 589832 | tf_op jit(solution)/shard_map/ppermute | solution.py:346
  33.0 9.9 %collective-permute-start.2 = (f32[24,16,128]{2,1,0:T(8,128)S(1)}, f32[24,16,128]{2,1,0:T(8,128)S(1)}, u32[]{:S(2)}, u32[]{:S(2)}) collective-permute-start(f32[24,16,128]{2,1,0:T(8,128)S(1)} %get-tuple-element.213), channel_id=1, source_target_pairs={{0,64},{16,80},{32,96},{48,112},{64,0},{80,16},{96,32},{112,48},{1... | collective-permute-start | bytes 589832 | tf_op jit(solution)/shard_map/ppermute | solution.py:346
  33.7 13.4 %collective-permute-start.1 = (f32[24,16,128]{2,1,0:T(8,128)S(1)}, f32[24,16,128]{2,1,0:T(8,128)S(1)}, u32[]{:S(2)}, u32[]{:S(2)}) collective-permute-start(f32[24,16,128]{2,1,0:T(8,128)S(1)} %get-tuple-element.214), channel_id=1, source_target_pairs={{0,32},{16,48},{32,64},{48,80},{64,96},{80,112},{96,0},{112,16},{1... | collective-permute-start | bytes 589832 | tf_op jit(solution)/shard_map/ppermute | solution.py:346
  61.2 39.5 %all-to-all-start = ((f32[4,36,16,128]{3,2,1,0:T(8,128)}), f32[4,36,16,128]{3,2,1,0:T(8,128)S(1)}, u32[]{:S(2)}, u32[]{:S(2)}) async-start(f32[4,36,16,128]{3,2,1,0:T(8,128)} %add.337), calls=%async_computation | async-start | bytes 2359296 | tf_op jit(solution)/shard_map/all_to_all | solution.py:382
  64.9 24.7 %collective-permute-start.7 = (f32[2,4,16,128]{3,2,1,0:T(8,128)S(1)}, f32[2,4,16,128]{3,2,1,0:T(8,128)S(1)}, u32[]{:S(2)}, u32[]{:S(2)}) collective-permute-start(f32[2,4,16,128]{3,2,1,0:T(8,128)S(1)} %copy-done.8), channel_id=1, source_target_pairs={{0,96},{16,112},{32,0},{48,16},{64,32},{80,48},{96,64},{112,80},{1... | collective-permute-start | bytes 196616 | tf_op jit(solution)/shard_map/ppermute | solution.py:346
  68.1 28.0 %collective-permute-start.10 = (f32[16,16,128]{2,1,0:T(8,128)S(1)}, f32[16,16,128]{2,1,0:T(8,128)S(1)}, u32[]{:S(2)}, u32[]{:S(2)}) collective-permute-start(f32[16,16,128]{2,1,0:T(8,128)S(1)} %slice.433.refs_4_), channel_id=1, source_target_pairs={{0,8},{1,9},{2,10},{3,11},{4,12},{5,13},{6,14},{7,15},{8,0},{9,1},... | collective-permute-start | bytes 393224 | tf_op jit(solution)/shard_map/ppermute | solution.py:344
  72.5 23.5 %collective-permute-start.9 = (f32[16,16,128]{2,1,0:T(8,128)S(1)}, f32[16,16,128]{2,1,0:T(8,128)S(1)}, u32[]{:S(2)}, u32[]{:S(2)}) collective-permute-start(f32[16,16,128]{2,1,0:T(8,128)S(1)} %slice.433.refs_4_), channel_id=1, source_target_pairs={{0,12},{1,13},{2,14},{3,15},{4,0},{5,1},{6,2},{7,3},{8,4},{9,5},{1... | collective-permute-start | bytes 393224 | tf_op jit(solution)/shard_map/ppermute | solution.py:344
  73.2 22.9 %collective-permute-start.8 = (f32[16,16,128]{2,1,0:T(8,128)S(1)}, f32[16,16,128]{2,1,0:T(8,128)S(1)}, u32[]{:S(2)}, u32[]{:S(2)}) collective-permute-start(f32[16,16,128]{2,1,0:T(8,128)S(1)} %slice.433.refs_4_), channel_id=1, source_target_pairs={{0,4},{1,5},{2,6},{3,7},{4,8},{5,9},{6,10},{7,11},{8,12},{9,13},{1... | collective-permute-start | bytes 393224 | tf_op jit(solution)/shard_map/ppermute | solution.py:344
  74.6 16.2 %collective-permute-start.6 = (f32[2,4,16,128]{3,2,1,0:T(8,128)S(1)}, f32[2,4,16,128]{3,2,1,0:T(8,128)S(1)}, u32[]{:S(2)}, u32[]{:S(2)}) collective-permute-start(f32[2,4,16,128]{3,2,1,0:T(8,128)S(1)} %copy-done.8), channel_id=1, source_target_pairs={{0,64},{16,80},{32,96},{48,112},{64,0},{80,16},{96,32},{112,48},{1... | collective-permute-start | bytes 196616 | tf_op jit(solution)/shard_map/ppermute | solution.py:346
  109.3 11.9 %collective-permute-start.22 = (f32[16,16,128]{2,1,0:T(8,128)S(1)}, f32[16,16,128]{2,1,0:T(8,128)S(1)}, u32[]{:S(2)}, u32[]{:S(2)}) collective-permute-start(f32[16,16,128]{2,1,0:T(8,128)S(1)} %slice.441), channel_id=1, source_target_pairs={{0,12},{1,13},{2,14},{3,15},{4,0},{5,1},{6,2},{7,3},{8,4},{9,5},{1... | collective-permute-start | bytes 393224 | tf_op jit(solution)/shard_map/ppermute | solution.py:344
  122.9 9.1 %collective-permute-start.23 = (f32[4,16,128]{2,1,0:T(8,128)S(1)}, f32[4,16,128]{2,1,0:T(8,128)S(1)}, u32[]{:S(2)}, u32[]{:S(2)}) collective-permute-start(f32[4,16,128]{2,1,0:T(8,128)S(1)} %get-tuple-element.166), channel_id=1, source_target_pairs={{0,1},{1,2},{2,3},{3,0},{4,5},{5,6},{6,7},{7,4},{8,9},{9,10},{10,1... | collective-permute-start | bytes 98312 | tf_op jit(solution)/shard_map/ppermute | solution.py:342
  128.7 9.7 %collective-permute-start.31 = (f32[48,16,128]{2,1,0:T(8,128)S(1)}, f32[48,16,128]{2,1,0:T(8,128)S(1)}, u32[]{:S(2)}, u32[]{:S(2)}) collective-permute-start(f32[48,16,128]{2,1,0:T(8,128)S(1)} %slice_bitcast_fusion.2.refs_6_), channel_id=1, source_target_pairs={{0,12},{1,13},{2,14},{3,15},{4,0},{5,1},{6,2},{7,3},{8,4},{9,5},{1... | collective-permute-start | bytes 1179656 | tf_op jit(solution)/shard_map/ppermute | solution.py:344
  132.0 9.7 %collective-permute-start.30 = (f32[48,16,128]{2,1,0:T(8,128)S(1)}, f32[48,16,128]{2,1,0:T(8,128)S(1)}, u32[]{:S(2)}, u32[]{:S(2)}) collective-permute-start(f32[48,16,128]{2,1,0:T(8,128)S(1)} %slice_bitcast_fusion.2.refs_6_), channel_id=1, source_target_pairs={{0,4},{1,5},{2,6},{3,7},{4,8},{5,9},{6,10},{7,11},{8,12},{9,13},{1... | collective-permute-start | bytes 1179656 | tf_op jit(solution)/shard_map/ppermute | solution.py:344
  133.2 36.3 %collective-permute-start.42 = (f32[64,16,128]{2,1,0:T(8,128)S(1)}, f32[64,16,128]{2,1,0:T(8,128)S(1)}, u32[]{:S(2)}, u32[]{:S(2)}) collective-permute-start(f32[64,16,128]{2,1,0:T(8,128)S(1)} %slice_bitcast_fusion.1.refs_7_), channel_id=1, source_target_pairs={{0,12},{1,13},{2,14},{3,15},{4,0},{5,1},{6,2},{7,3},{8,4},{9,5},{1... | collective-permute-start | bytes 1572872 | tf_op jit(solution)/shard_map/ppermute | solution.py:344
  136.5 33.1 %collective-permute-start.41 = (f32[64,16,128]{2,1,0:T(8,128)S(1)}, f32[64,16,128]{2,1,0:T(8,128)S(1)}, u32[]{:S(2)}, u32[]{:S(2)}) collective-permute-start(f32[64,16,128]{2,1,0:T(8,128)S(1)} %slice_bitcast_fusion.1.refs_7_), channel_id=1, source_target_pairs={{0,4},{1,5},{2,6},{3,7},{4,8},{5,9},{6,10},{7,11},{8,12},{9,13},{1... | collective-permute-start | bytes 1572872 | tf_op jit(solution)/shard_map/ppermute | solution.py:344
  138.4 14.8 %collective-permute-start.33 = (f32[24,16,128]{2,1,0:T(8,128)S(1)}, f32[24,16,128]{2,1,0:T(8,128)S(1)}, u32[]{:S(2)}, u32[]{:S(2)}) collective-permute-start(f32[24,16,128]{2,1,0:T(8,128)S(1)} %slice.445), channel_id=1, source_target_pairs={{0,12},{1,13},{2,14},{3,15},{4,0},{5,1},{6,2},{7,3},{8,4},{9,5},{1... | collective-permute-start | bytes 589832 | tf_op jit(solution)/shard_map/ppermute | solution.py:344
  141.7 14.7 %collective-permute-start.32 = (f32[24,16,128]{2,1,0:T(8,128)S(1)}, f32[24,16,128]{2,1,0:T(8,128)S(1)}, u32[]{:S(2)}, u32[]{:S(2)}) collective-permute-start(f32[24,16,128]{2,1,0:T(8,128)S(1)} %slice.444), channel_id=1, source_target_pairs={{0,4},{1,5},{2,6},{3,7},{4,8},{5,9},{6,10},{7,11},{8,12},{9,13},{1... | collective-permute-start | bytes 589832 | tf_op jit(solution)/shard_map/ppermute | solution.py:344
  169.6 11.2 %collective-permute-start.44 = (f32[32,16,128]{2,1,0:T(8,128)S(1)}, f32[32,16,128]{2,1,0:T(8,128)S(1)}, u32[]{:S(2)}, u32[]{:S(2)}) collective-permute-start(f32[32,16,128]{2,1,0:T(8,128)S(1)} %slice.449), channel_id=1, source_target_pairs={{0,12},{1,13},{2,14},{3,15},{4,0},{5,1},{6,2},{7,3},{8,4},{9,5},{1... | collective-permute-start | bytes 786440 | tf_op jit(solution)/shard_map/ppermute | solution.py:344
  170.4 10.4 %collective-permute-start.43 = (f32[32,16,128]{2,1,0:T(8,128)}, f32[32,16,128]{2,1,0:T(8,128)S(1)}, u32[]{:S(2)}, u32[]{:S(2)}) collective-permute-start(f32[32,16,128]{2,1,0:T(8,128)} %slice.448), channel_id=1, source_target_pairs={{0,4},{1,5},{2,6},{3,7},{4,8},{5,9},{6,10},{7,11},{8,12},{9,13},{1... | collective-permute-start | bytes 786440 | tf_op jit(solution)/shard_map/ppermute | solution.py:344
  177.1 15.3 %collective-permute-start.53 = (f32[80,16,128]{2,1,0:T(8,128)S(1)}, f32[80,16,128]{2,1,0:T(8,128)S(1)}, u32[]{:S(2)}, u32[]{:S(2)}) collective-permute-start(f32[80,16,128]{2,1,0:T(8,128)S(1)} %slice_bitcast_fusion.refs_8_), channel_id=1, source_target_pairs={{0,12},{1,13},{2,14},{3,15},{4,0},{5,1},{6,2},{7,3},{8,4},{9,5},{1... | collective-permute-start | bytes 1966088 | tf_op jit(solution)/shard_map/ppermute | solution.py:344
  180.1 16.3 %collective-permute-start.52 = (f32[80,16,128]{2,1,0:T(8,128)S(1)}, f32[80,16,128]{2,1,0:T(8,128)S(1)}, u32[]{:S(2)}, u32[]{:S(2)}) collective-permute-start(f32[80,16,128]{2,1,0:T(8,128)S(1)} %slice_bitcast_fusion.refs_8_), channel_id=1, source_target_pairs={{0,4},{1,5},{2,6},{3,7},{4,8},{5,9},{6,10},{7,11},{8,12},{9,13},{1... | collective-permute-start | bytes 1966088 | tf_op jit(solution)/shard_map/ppermute | solution.py:344
  192.5 8.6 %collective-permute-start.55 = (f32[40,16,128]{2,1,0:T(8,128)S(1)}, f32[40,16,128]{2,1,0:T(8,128)S(1)}, u32[]{:S(2)}, u32[]{:S(2)}) collective-permute-start(f32[40,16,128]{2,1,0:T(8,128)S(1)} %slice.453), channel_id=1, source_target_pairs={{0,12},{1,13},{2,14},{3,15},{4,0},{5,1},{6,2},{7,3},{8,4},{9,5},{1... | collective-permute-start | bytes 983048 | tf_op jit(solution)/shard_map/ppermute | solution.py:344
  216.2 9.0 %collective-permute-start.64 = (f32[16,128]{1,0:T(8,128)S(1)}, f32[16,128]{1,0:T(8,128)S(1)}, u32[]{:S(2)}, u32[]{:S(2)}) collective-permute-start(f32[16,128]{1,0:T(8,128)S(1)} %get-tuple-element.235), channel_id=1, source_target_pairs={{0,12},{1,13},{2,14},{3,15},{4,0},{5,1},{6,2},{7,3},{8,4},{9,5},{1... | collective-permute-start | bytes 24584 | tf_op jit(solution)/shard_map/ppermute | solution.py:344
  220.6 18.6 %collective-permute-start.58 = (f32[5,128,128]{2,1,0:T(8,128)S(1)}, f32[5,128,128]{2,1,0:T(8,128)S(1)}, u32[]{:S(2)}, u32[]{:S(2)}) collective-permute-start(f32[5,128,128]{2,1,0:T(8,128)S(1)} %get-tuple-element.215), channel_id=1, source_target_pairs={{0,12},{1,13},{2,14},{3,15},{4,0},{5,1},{6,2},{7,3},{8,4},{9,5},{1... | collective-permute-start | bytes 983048 | tf_op jit(solution)/shard_map/ppermute | solution.py:344
  222.9 16.4 %collective-permute-start.57 = (f32[5,128,128]{2,1,0:T(8,128)}, f32[5,128,128]{2,1,0:T(8,128)S(1)}, u32[]{:S(2)}, u32[]{:S(2)}) collective-permute-start(f32[5,128,128]{2,1,0:T(8,128)} %get-tuple-element.216), channel_id=1, source_target_pairs={{0,8},{1,9},{2,10},{3,11},{4,12},{5,13},{6,14},{7,15},{8,0},{9,1},... | collective-permute-start | bytes 983048 | tf_op jit(solution)/shard_map/ppermute | solution.py:344
  225.2 14.0 %collective-permute-start.56 = (f32[5,128,128]{2,1,0:T(8,128)}, f32[5,128,128]{2,1,0:T(8,128)S(1)}, u32[]{:S(2)}, u32[]{:S(2)}) collective-permute-start(f32[5,128,128]{2,1,0:T(8,128)} %get-tuple-element.217), channel_id=1, source_target_pairs={{0,4},{1,5},{2,6},{3,7},{4,8},{5,9},{6,10},{7,11},{8,12},{9,13},{1... | collective-permute-start | bytes 983048 | tf_op jit(solution)/shard_map/ppermute | solution.py:344
  248.7 20.5 %collective-permute-start.75 = (f32[1,256,512]{2,1,0:T(8,128)}, f32[1,256,512]{2,1,0:T(8,128)}, u32[]{:S(2)}, u32[]{:S(2)}) collective-permute-start(f32[1,256,512]{2,1,0:T(8,128)} %get-tuple-element.197), channel_id=1, source_target_pairs={{0,12},{1,13},{2,14},{3,15},{4,0},{5,1},{6,2},{7,3},{8,4},{9,5},{1... | collective-permute-start | bytes 1572872 | tf_op jit(solution)/shard_map/ppermute | solution.py:344
  251.2 22.7 %collective-permute-start.73 = (f32[1,256,512]{2,1,0:T(8,128)}, f32[1,256,512]{2,1,0:T(8,128)S(1)}, u32[]{:S(2)}, u32[]{:S(2)}) collective-permute-start(f32[1,256,512]{2,1,0:T(8,128)} %get-tuple-element.195), channel_id=1, source_target_pairs={{0,4},{1,5},{2,6},{3,7},{4,8},{5,9},{6,10},{7,11},{8,12},{9,13},{1... | collective-permute-start | bytes 1572872 | tf_op jit(solution)/shard_map/ppermute | solution.py:344
  251.3 22.8 %collective-permute-start.71 = (f32[1,256,512]{2,1,0:T(8,128)}, f32[1,256,512]{2,1,0:T(8,128)S(1)}, u32[]{:S(2)}, u32[]{:S(2)}) collective-permute-start(f32[1,256,512]{2,1,0:T(8,128)} %get-tuple-element.192), channel_id=1, source_target_pairs={{0,3},{1,0},{2,1},{3,2},{4,7},{5,4},{6,5},{7,6},{8,11},{9,8},{10,9... | collective-permute-start | bytes 1572872 | tf_op jit(solution)/shard_map/ppermute | solution.py:342
  252.2 22.2 %collective-permute-start.69 = (f32[1,256,512]{2,1,0:T(8,128)}, f32[1,256,512]{2,1,0:T(8,128)S(1)}, u32[]{:S(2)}, u32[]{:S(2)}) collective-permute-start(f32[1,256,512]{2,1,0:T(8,128)} %get-tuple-element.188._), channel_id=1, source_target_pairs={{0,1},{1,2},{2,3},{3,0},{4,5},{5,6},{6,7},{7,4},{8,9},{9,10},{10,1... | collective-permute-start | bytes 1572872 | tf_op jit(solution)/shard_map/ppermute | solution.py:342
  270.4 22.5 %collective-permute-start.76 = (f32[2,256,512]{2,1,0:T(8,128)S(1)}, f32[2,256,512]{2,1,0:T(8,128)S(1)}, u32[]{:S(2)}, u32[]{:S(2)}) collective-permute-start(f32[2,256,512]{2,1,0:T(8,128)S(1)} %add_dynamic-update-slice_fusion), channel_id=1, source_target_pairs={{0,12},{1,13},{2,14},{3,15},{4,0},{5,1},{6,2},{7,3},{8,4},{9,5},{1... | collective-permute-start | bytes 3145736 | tf_op jit(solution)/shard_map/ppermute | solution.py:344
  274.1 22.5 %collective-permute-start.74 = (f32[2,256,512]{2,1,0:T(8,128)S(1)}, f32[2,256,512]{2,1,0:T(8,128)S(1)}, u32[]{:S(2)}, u32[]{:S(2)}) collective-permute-start(f32[2,256,512]{2,1,0:T(8,128)S(1)} %add_dynamic-update-slice_fusion.1), channel_id=1, source_target_pairs={{0,4},{1,5},{2,6},{3,7},{4,8},{5,9},{6,10},{7,11},{8,12},{9,13},{1... | collective-permute-start | bytes 3145736 | tf_op jit(solution)/shard_map/ppermute | solution.py:344
  274.3 22.5 %collective-permute-start.72 = (f32[2,256,512]{2,1,0:T(8,128)S(1)}, f32[2,256,512]{2,1,0:T(8,128)S(1)}, u32[]{:S(2)}, u32[]{:S(2)}) collective-permute-start(f32[2,256,512]{2,1,0:T(8,128)S(1)} %add_dynamic-update-slice_fusion.2), channel_id=1, source_target_pairs={{0,3},{1,0},{2,1},{3,2},{4,7},{5,4},{6,5},{7,6},{8,11},{9,8},{10,9... | collective-permute-start | bytes 3145736 | tf_op jit(solution)/shard_map/ppermute | solution.py:342
  274.5 22.3 %collective-permute-start.70 = (f32[2,256,512]{2,1,0:T(8,128)S(1)}, f32[2,256,512]{2,1,0:T(8,128)S(1)}, u32[]{:S(2)}, u32[]{:S(2)}) collective-permute-start(f32[2,256,512]{2,1,0:T(8,128)S(1)} %add_dynamic-update-slice_fusion.3), channel_id=1, source_target_pairs={{0,1},{1,2},{2,3},{3,0},{4,5},{5,6},{6,7},{7,4},{8,9},{9,10},{10,1... | collective-permute-start | bytes 3145736 | tf_op jit(solution)/shard_map/ppermute | solution.py:342
  299.1 15.7 %collective-permute-start.77 = (f32[64,512]{1,0:T(8,128)S(1)}, f32[64,512]{1,0:T(8,128)S(1)}, u32[]{:S(2)}, u32[]{:S(2)}) collective-permute-start(f32[64,512]{1,0:T(8,128)S(1)} %get-tuple-element.200), channel_id=1, source_target_pairs={{0,4},{1,5},{2,6},{3,7},{4,8},{5,9},{6,10},{7,11},{8,12},{9,13},{1... | collective-permute-start | bytes 393224 | tf_op jit(solution)/shard_map/ppermute | solution.py:344
  299.1 14.1 %collective-permute-start.79 = (f32[64,512]{1,0:T(8,128)S(1)}, f32[64,512]{1,0:T(8,128)S(1)}, u32[]{:S(2)}, u32[]{:S(2)}) collective-permute-start(f32[64,512]{1,0:T(8,128)S(1)} %get-tuple-element.202), channel_id=1, source_target_pairs={{0,12},{1,13},{2,14},{3,15},{4,0},{5,1},{6,2},{7,3},{8,4},{9,5},{1... | collective-permute-start | bytes 393224 | tf_op jit(solution)/shard_map/ppermute | solution.py:344
  306.7 9.4 %collective-permute-start.84 = (f32[128,512]{1,0:T(8,128)S(1)}, f32[128,512]{1,0:T(8,128)S(1)}, u32[]{:S(2)}, u32[]{:S(2)}) collective-permute-start(f32[128,512]{1,0:T(8,128)S(1)} %add_dynamic-update-slice_fusion.4), channel_id=1, source_target_pairs={{0,3},{1,0},{2,1},{3,2},{4,7},{5,4},{6,5},{7,6},{8,11},{9,8},{10,9... | collective-permute-start | bytes 786440 | tf_op jit(solution)/shard_map/ppermute | solution.py:342
  314.8 9.0 %collective-permute-start.78 = (f32[128,512]{1,0:T(8,128)S(1)}, f32[128,512]{1,0:T(8,128)S(1)}, u32[]{:S(2)}, u32[]{:S(2)}) collective-permute-start(f32[128,512]{1,0:T(8,128)S(1)} %add_dynamic-update-slice_fusion.7), channel_id=1, source_target_pairs={{0,4},{1,5},{2,6},{3,7},{4,8},{5,9},{6,10},{7,11},{8,12},{9,13},{1... | collective-permute-start | bytes 786440 | tf_op jit(solution)/shard_map/ppermute | solution.py:344
  348.0 20.5 %collective-permute-start.99 = (f32[2,256,512]{2,1,0:T(8,128)S(1)}, f32[2,256,512]{2,1,0:T(8,128)S(1)}, u32[]{:S(2)}, u32[]{:S(2)}) collective-permute-start(f32[2,256,512]{2,1,0:T(8,128)S(1)} %bitcast.111), channel_id=1, source_target_pairs={{0,12},{1,13},{2,14},{3,15},{4,0},{5,1},{6,2},{7,3},{8,4},{9,5},{1... | collective-permute-start | bytes 3145736 | tf_op jit(solution)/shard_map/ppermute | solution.py:344
  349.4 22.5 %collective-permute-start.97 = (f32[2,256,512]{2,1,0:T(8,128)S(1)}, f32[2,256,512]{2,1,0:T(8,128)S(1)}, u32[]{:S(2)}, u32[]{:S(2)}) collective-permute-start(f32[2,256,512]{2,1,0:T(8,128)S(1)} %bitcast.112), channel_id=1, source_target_pairs={{0,4},{1,5},{2,6},{3,7},{4,8},{5,9},{6,10},{7,11},{8,12},{9,13},{1... | collective-permute-start | bytes 3145736 | tf_op jit(solution)/shard_map/ppermute | solution.py:344
  350.1 22.8 %collective-permute-start.95 = (f32[2,256,512]{2,1,0:T(8,128)S(1)}, f32[2,256,512]{2,1,0:T(8,128)S(1)}, u32[]{:S(2)}, u32[]{:S(2)}) collective-permute-start(f32[2,256,512]{2,1,0:T(8,128)S(1)} %bitcast.108), channel_id=1, source_target_pairs={{0,3},{1,0},{2,1},{3,2},{4,7},{5,4},{6,5},{7,6},{8,11},{9,8},{10,9... | collective-permute-start | bytes 3145736 | tf_op jit(solution)/shard_map/ppermute | solution.py:342
  350.1 23.8 %collective-permute-start.93 = (f32[2,256,512]{2,1,0:T(8,128)S(1)}, f32[2,256,512]{2,1,0:T(8,128)S(1)}, u32[]{:S(2)}, u32[]{:S(2)}) collective-permute-start(f32[2,256,512]{2,1,0:T(8,128)S(1)} %bitcast.109), channel_id=1, source_target_pairs={{0,1},{1,2},{2,3},{3,0},{4,5},{5,6},{6,7},{7,4},{8,9},{9,10},{10,1... | collective-permute-start | bytes 3145736 | tf_op jit(solution)/shard_map/ppermute | solution.py:342
  369.4 204.1 %collective-permute-start.100 = (f32[1,256,512]{2,1,0:T(8,128)}, f32[1,256,512]{2,1,0:T(8,128)S(1)}, u32[]{:S(2)}, u32[]{:S(2)}) collective-permute-start(f32[1,256,512]{2,1,0:T(8,128)} %slice.466), channel_id=1, source_target_pairs={{0,12},{1,13},{2,14},{3,15},{4,0},{5,1},{6,2},{7,3},{8,4},{9,5},{1... | collective-permute-start | bytes 1572872 | tf_op jit(solution)/shard_map/ppermute | solution.py:344
  372.9 200.6 %collective-permute-start.98 = (f32[1,256,512]{2,1,0:T(8,128)}, f32[1,256,512]{2,1,0:T(8,128)S(1)}, u32[]{:S(2)}, u32[]{:S(2)}) collective-permute-start(f32[1,256,512]{2,1,0:T(8,128)} %slice.465), channel_id=1, source_target_pairs={{0,4},{1,5},{2,6},{3,7},{4,8},{5,9},{6,10},{7,11},{8,12},{9,13},{1... | collective-permute-start | bytes 1572872 | tf_op jit(solution)/shard_map/ppermute | solution.py:344
  373.8 199.8 %collective-permute-start.96 = (f32[1,256,512]{2,1,0:T(8,128)}, f32[1,256,512]{2,1,0:T(8,128)S(1)}, u32[]{:S(2)}, u32[]{:S(2)}) collective-permute-start(f32[1,256,512]{2,1,0:T(8,128)} %slice.464), channel_id=1, source_target_pairs={{0,3},{1,0},{2,1},{3,2},{4,7},{5,4},{6,5},{7,6},{8,11},{9,8},{10,9... | collective-permute-start | bytes 1572872 | tf_op jit(solution)/shard_map/ppermute | solution.py:342
  375.3 198.3 %collective-permute-start.94 = (f32[1,256,512]{2,1,0:T(8,128)}, f32[1,256,512]{2,1,0:T(8,128)}, u32[]{:S(2)}, u32[]{:S(2)}) collective-permute-start(f32[1,256,512]{2,1,0:T(8,128)} %slice.463), channel_id=1, source_target_pairs={{0,1},{1,2},{2,3},{3,0},{4,5},{5,6},{6,7},{7,4},{8,9},{9,10},{10,1... | collective-permute-start | bytes 1572872 | tf_op jit(solution)/shard_map/ppermute | solution.py:342
  (90 other events, 531.1 us)
Sparse Core Ops, SparseCore 0:
  28.9 70.4 reduce-scatter.2
  101.8 42.9 reduce-scatter.4
